TPU v7x, 32 devices: a whole 2x2x4 slice. The times are simulated.
32 devices in a mesh: dp: 8 (over y, x, core), tensor: 4 (over z).
Axes of the slice: x: 2, y: 2, z: 4, core: 2. Of those that a mesh axis runs over, the one named last changes fastest.
Arguments:
- tokens: bfloat16 [4096, 768], P(('dp', 'tensor')), may hold values from -6 to 6
- norm_gain_pair: float32 [2, 768], P(None, ('dp', 'tensor')), may hold values from 0.5 to 1.5
- norm_bias_pair: float32 [2, 768], P(None, ('dp', 'tensor')), may hold values from -3 to 3
- w_qkv: bfloat16 [3, 768, 768], P(None, 'dp', 'tensor'), may hold values from -0.21875 to 0.21875
- qv_bias: float32 [2, 768], P(None, ('dp', 'tensor')), may hold values from -3 to 3
- w_out: bfloat16 [768, 768], P('tensor', 'dp'), may hold values from -0.875 to 0.875
- res_bias: float32 [2, 768], P(None, ('dp', 'tensor')), may hold values from -3 to 3
- w_fc: bfloat16 [768, 3072], P('dp', 'tensor'), may hold values from -0.21875 to 0.21875
- fc_bias: float32 [3072], P(('dp', 'tensor')), may hold values from -3 to 3
- w_proj: bfloat16 [3072, 768], P('tensor', 'dp'), may hold values from -0.109375 to 0.109375
- segments: int32 [8, 512], P('dp'), may hold values from 0 to 3, never falling along the last dimension, each value on 1 to 256 neighbouring positions
- cotangent: bfloat16 [4096, 768], P(('dp', 'tensor')), may hold values from -6 to 6
Outputs:
- block_out: bfloat16 [4096, 768], P(('dp', 'tensor'))
- block_input_gradient: bfloat16 [4096, 768], P(('dp', 'tensor'))
- ln_gain_grad: float32 [2, 768], P(None, ('dp', 'tensor'))
- ln_bias_grad: float32 [2, 768], P(None, ('dp', 'tensor'))
- w_qkv_grad: float32 [3, 768, 768], P(None, 'dp', 'tensor')
- qv_bias_grad: float32 [2, 768], P(None, ('dp', 'tensor'))
- w_out_grad: float32 [768, 768], P('tensor', 'dp')
- res_bias_grad: float32 [2, 768], P(None, ('dp', 'tensor'))
- w_fc_grad: float32 [768, 3072], P('dp', 'tensor')
- fc_bias_grad: float32 [3072], P(('dp', 'tensor'))
- w_proj_grad: float32 [3072, 768], P('tensor', 'dp')
Inputs may be any that keep to these rules, and one draw needn't show every extreme that they name: `segments`: in each sequence the document numbers never fall, so every document is a contiguous run of tokens.
All inputs are finite; a program needn't handle non-finite values.
Results may differ from a plain program's by a relative error of at most 0.012.
Values may be sent and summed in bfloat16 or wider, within the bound.
A program may use at most 64 MiB of HBM per device.

v0:
```python
import jax
import jax.numpy as jnp
from jax import lax
from jax.sharding import PartitionSpec as P

HEAD_DIM = 64


epsilon = 1e-05
gelu_coeff = 0.044715
gelu_root = 0.7978845608028654


def layer_normalize(rows, norm_gain, norm_shift):
    centered_input = rows - jnp.mean(rows, axis=-1, keepdims=True)
    inverse_deviation = lax.rsqrt(
        jnp.mean(centered_input * centered_input, axis=-1, keepdims=True) + epsilon
    )
    standardized_input = centered_input * inverse_deviation
    return (standardized_input * norm_gain + norm_shift, standardized_input, inverse_deviation)


def layer_normalize_backward(output_gradient, standardized_input, inverse_deviation, norm_gain):
    scaled_rows = output_gradient * norm_gain
    return inverse_deviation * (
        scaled_rows
        - jnp.mean(scaled_rows, axis=-1, keepdims=True)
        - standardized_input * jnp.mean(scaled_rows * standardized_input, axis=-1, keepdims=True)
    )


def gelu_value(pre):
    return 0.5 * pre * (1.0 + jnp.tanh(gelu_root * (pre + gelu_coeff * pre * pre * pre)))


def gelu_slope(pre):
    tangent = jnp.tanh(gelu_root * (pre + gelu_coeff * pre * pre * pre))
    return 0.5 * (1.0 + tangent) + 0.5 * pre * (1.0 - tangent * tangent) * gelu_root * (
        1.0 + 3.0 * gelu_coeff * pre * pre
    )


def allowed_pairs(segment):
    length = segment.shape[0]
    rows = lax.broadcasted_iota(jnp.int32, (length, length), 0)
    cols = lax.broadcasted_iota(jnp.int32, (length, length), 1)
    return (segment[:, None] == segment[None, :]) & (rows >= cols)


def masked_scores(query, key, segment):
    scores = jnp.einsum(
        "qhd,khd->hqk", query, key, preferred_element_type=jnp.float32
    ) * HEAD_DIM ** (-0.5)
    return jnp.where(allowed_pairs(segment)[None], scores, -1e30)


def attend(pieces):
    query, key, value, segment = pieces
    scores = masked_scores(query, key, segment)
    peak = jnp.max(scores, axis=-1, keepdims=True)
    logsum = peak + jnp.log(jnp.sum(jnp.exp(scores - peak), axis=-1, keepdims=True))
    weights = jnp.exp(scores - logsum).astype(jnp.bfloat16)
    context = jnp.einsum("hqk,khd->qhd", weights, value, preferred_element_type=jnp.float32)
    return (context.astype(jnp.bfloat16), logsum)


def attend_back(pieces):
    query, key, value, segment, logsum, grad_context = pieces
    probs = jnp.exp(masked_scores(query, key, segment) - logsum)
    probs_half = probs.astype(jnp.bfloat16)
    grad_value = jnp.einsum(
        "hqk,qhd->khd", probs_half, grad_context, preferred_element_type=jnp.float32
    )
    grad_probs = jnp.einsum("qhd,khd->hqk", grad_context, value, preferred_element_type=jnp.float32)
    inner = jnp.sum(probs * grad_probs, axis=-1, keepdims=True)
    grad_scores = (probs * (grad_probs - inner)).astype(jnp.bfloat16)
    grad_query = jnp.einsum(
        "hqk,khd->qhd", grad_scores, key, preferred_element_type=jnp.float32
    ) * HEAD_DIM ** (-0.5)
    grad_key = jnp.einsum(
        "hqk,qhd->khd", grad_scores, query, preferred_element_type=jnp.float32
    ) * HEAD_DIM ** (-0.5)
    return (grad_query, grad_key, grad_value)


def contract_rows(left, right):
    return lax.dot_general(
        left, right, (((0,), (0,)), ((), ())), preferred_element_type=jnp.float32
    )


def contract_cols(left, right):
    return lax.dot_general(
        left, right, (((1,), (1,)), ((), ())), preferred_element_type=jnp.float32
    )


def shards(
    tokens,
    norm_gain_pair,
    norm_bias_pair,
    w_qkv,
    qv_bias,
    w_out,
    res_bias,
    w_fc,
    fc_bias,
    w_proj,
    segments,
    cotangent,
):
    place = lax.axis_index("tensor")
    width = tokens.shape[1]
    local_width = w_qkv.shape[2]
    local_hidden = w_fc.shape[1]
    seqs = segments.shape[0]
    length = segments.shape[1]
    heads_local = local_width // HEAD_DIM
    head_start = place * local_width
    hidden_start = place * local_hidden
    norm_gains, norm_shifts, qv_whole, res_whole, fc_whole = (
        lax.all_gather(norm_gain_pair, ("dp", "tensor"), axis=1, tiled=True),
        lax.all_gather(norm_bias_pair, ("dp", "tensor"), axis=1, tiled=True),
        lax.all_gather(qv_bias, ("dp", "tensor"), axis=1, tiled=True),
        lax.all_gather(res_bias, ("dp", "tensor"), axis=1, tiled=True),
        lax.all_gather(fc_bias, ("dp", "tensor"), axis=0, tiled=True),
    )
    qv_local = lax.dynamic_slice_in_dim(qv_whole, head_start, local_width, 1)
    fc_local = lax.dynamic_slice_in_dim(fc_whole, hidden_start, local_hidden, 0)
    qkv_full, out_full, fc_full, proj_full = (
        lax.all_gather(w_qkv, "dp", axis=1, tiled=True),
        lax.all_gather(w_out, "dp", axis=1, tiled=True),
        lax.all_gather(w_fc, "dp", axis=0, tiled=True),
        lax.all_gather(w_proj, "dp", axis=1, tiled=True),
    )
    residual_stream = tokens.astype(jnp.float32)
    first_norm_output, first_standardized, first_inverse_deviation = layer_normalize(
        residual_stream, norm_gains[0], norm_shifts[0]
    )
    ln1_all, cot_all = (
        lax.all_gather(first_norm_output.astype(jnp.bfloat16), "tensor", axis=0, tiled=True),
        lax.all_gather(cotangent, "tensor", axis=0, tiled=True),
    )
    rows_all = ln1_all.shape[0]
    query = (
        jnp.dot(ln1_all, qkv_full[0], preferred_element_type=jnp.float32) + qv_local[0]
    ).astype(jnp.bfloat16)
    keys = jnp.dot(ln1_all, qkv_full[1], preferred_element_type=jnp.float32).astype(jnp.bfloat16)
    value = (
        jnp.dot(ln1_all, qkv_full[2], preferred_element_type=jnp.float32) + qv_local[1]
    ).astype(jnp.bfloat16)

    def split(array):
        return array.reshape(seqs, length, heads_local, HEAD_DIM)

    context, logsum = lax.map(attend, (split(query), split(keys), split(value), segments))
    context = context.reshape(rows_all, local_width)
    first_hidden = (
        residual_stream
        + lax.psum_scatter(
            jnp.dot(context, out_full, preferred_element_type=jnp.float32),
            "tensor",
            scatter_dimension=0,
            tiled=True,
        )
        + res_whole[0]
    )
    second_norm_output, second_standardized, second_inverse_deviation = layer_normalize(
        first_hidden, norm_gains[1], norm_shifts[1]
    )
    ln2_all = lax.all_gather(second_norm_output.astype(jnp.bfloat16), "tensor", axis=0, tiled=True)
    pre = jnp.dot(ln2_all, fc_full, preferred_element_type=jnp.float32) + fc_local
    act = gelu_value(pre).astype(jnp.bfloat16)
    block_out = (
        first_hidden
        + lax.psum_scatter(
            jnp.dot(act, proj_full, preferred_element_type=jnp.float32),
            "tensor",
            scatter_dimension=0,
            tiled=True,
        )
        + res_whole[1]
    ).astype(jnp.bfloat16)
    qkv_full, out_full, fc_full, proj_full = (
        lax.all_gather(w_qkv, "dp", axis=1, tiled=True),
        lax.all_gather(w_out, "dp", axis=1, tiled=True),
        lax.all_gather(w_fc, "dp", axis=0, tiled=True),
        lax.all_gather(w_proj, "dp", axis=1, tiled=True),
    )
    residual_gradient = cotangent.astype(jnp.float32)
    proj_grad = contract_rows(act, cot_all)
    res1_grad = jnp.sum(residual_gradient, axis=0)
    d_pre = contract_cols(cot_all, proj_full) * gelu_slope(pre)
    fcb_grad = jnp.sum(d_pre, axis=0)
    d_pre_half = d_pre.astype(jnp.bfloat16)
    fc_grad = contract_rows(ln2_all, d_pre_half)
    second_norm_gradient = lax.psum_scatter(
        contract_cols(d_pre_half, fc_full), "tensor", scatter_dimension=0, tiled=True
    )
    second_gain_gradient = jnp.sum(second_norm_gradient * second_standardized, axis=0)
    shift2_grad = jnp.sum(second_norm_gradient, axis=0)
    first_hidden_gradient = residual_gradient + layer_normalize_backward(
        second_norm_gradient, second_standardized, second_inverse_deviation, norm_gains[1]
    )
    res0_grad = jnp.sum(first_hidden_gradient, axis=0)
    d_hidden_all = lax.all_gather(
        first_hidden_gradient.astype(jnp.bfloat16), "tensor", axis=0, tiled=True
    )
    out_grad = contract_rows(context, d_hidden_all)
    d_context = contract_cols(d_hidden_all, out_full).astype(jnp.bfloat16)
    grad_query, grad_key, grad_value = lax.map(
        attend_back, (split(query), split(keys), split(value), segments, logsum, split(d_context))
    )
    grad_query = grad_query.reshape(rows_all, local_width)
    grad_key = grad_key.reshape(rows_all, local_width)
    grad_value = grad_value.reshape(rows_all, local_width)
    qb_grad = jnp.sum(grad_query, axis=0)
    vb_grad = jnp.sum(grad_value, axis=0)
    d_qkv = jnp.stack([grad_query, grad_key, grad_value]).astype(jnp.bfloat16)
    qkv_grad = jnp.einsum("td,itw->idw", ln1_all, d_qkv, preferred_element_type=jnp.float32)
    first_norm_gradient = lax.psum_scatter(
        jnp.einsum("itw,idw->td", d_qkv, qkv_full, preferred_element_type=jnp.float32),
        "tensor",
        scatter_dimension=0,
        tiled=True,
    )
    first_gain_gradient = jnp.sum(first_norm_gradient * first_standardized, axis=0)
    shift1_grad = jnp.sum(first_norm_gradient, axis=0)
    block_input_gradient = (
        first_hidden_gradient
        + layer_normalize_backward(
            first_norm_gradient, first_standardized, first_inverse_deviation, norm_gains[0]
        )
    ).astype(jnp.bfloat16)
    qkv_part, out_part, fc_part, proj_part = (
        lax.psum_scatter(qkv_grad, "dp", scatter_dimension=1, tiled=True),
        lax.psum_scatter(out_grad, "dp", scatter_dimension=1, tiled=True),
        lax.psum_scatter(fc_grad, "dp", scatter_dimension=0, tiled=True),
        lax.psum_scatter(proj_grad, "dp", scatter_dimension=1, tiled=True),
    )
    qv_spread = lax.dynamic_update_slice(
        jnp.zeros((2, width), jnp.float32), jnp.stack([qb_grad, vb_grad]), (0, head_start)
    )
    fc_spread = lax.dynamic_update_slice(
        jnp.zeros((fc_whole.shape[0],), jnp.float32), fcb_grad, (hidden_start,)
    )
    gain_part, shift_part, qv_part, res_part, fcb_part = (
        lax.psum_scatter(
            jnp.stack([first_gain_gradient, second_gain_gradient]),
            ("dp", "tensor"),
            scatter_dimension=1,
            tiled=True,
        ),
        lax.psum_scatter(
            jnp.stack([shift1_grad, shift2_grad]), ("dp", "tensor"), scatter_dimension=1, tiled=True
        ),
        lax.psum_scatter(qv_spread, ("dp", "tensor"), scatter_dimension=1, tiled=True),
        lax.psum_scatter(
            jnp.stack([res0_grad, res1_grad]), ("dp", "tensor"), scatter_dimension=1, tiled=True
        ),
        lax.psum_scatter(fc_spread, ("dp", "tensor"), scatter_dimension=0, tiled=True),
    )
    return (
        block_out,
        block_input_gradient,
        gain_part,
        shift_part,
        qkv_part,
        qv_part,
        out_part,
        res_part,
        fc_part,
        fcb_part,
        proj_part,
    )


def solution(mesh):
    return jax.shard_map(
        shards,
        mesh=mesh,
        in_specs=(
            P(("dp", "tensor"), None),
            P(None, ("dp", "tensor")),
            P(None, ("dp", "tensor")),
            P(None, "dp", "tensor"),
            P(None, ("dp", "tensor")),
            P("tensor", "dp"),
            P(None, ("dp", "tensor")),
            P("dp", "tensor"),
            P(("dp", "tensor")),
            P("tensor", "dp"),
            P("dp", None),
            P(("dp", "tensor"), None),
        ),
        out_specs=(
            P(("dp", "tensor"), None),
            P(("dp", "tensor"), None),
            P(None, ("dp", "tensor")),
            P(None, ("dp", "tensor")),
            P(None, "dp", "tensor"),
            P(None, ("dp", "tensor")),
            P("tensor", "dp"),
            P(None, ("dp", "tensor")),
            P("dp", "tensor"),
            P(("dp", "tensor")),
            P("tensor", "dp"),
        ),
        check_vma=False,
    )
```

profile of v0, /device:TPU:0, one launch (start us, length us, event | category | flops | bytes accessed | tf_op | source)
XLA Modules:
  0.0 723.6 jit_solution(11468512077972892987)
XLA Ops:
  10.4 70.0 %all-gather = f32[32,24,2]{1,2,0:T(2,128)S(1)} all-gather(f32[1,24,2]{1,2,0:T(2,128)} %bitcast.127), channel_id=1, replica_groups=mesh['dp'=8,'tensor'=4] {'dp','tensor'}, dimensions={0}, use_global_device_ids=true | all-gather | bytes 6336 | tf_op jit(solution)/shard_map/all_gather | solution.py:122
  80.6 63.8 %all-gather.1 = f32[32,24,2]{1,2,0:T(2,128)S(1)} all-gather(f32[1,24,2]{1,2,0:T(2,128)} %bitcast.128), channel_id=1, replica_groups=mesh['dp'=8,'tensor'=4] {'dp','tensor'}, dimensions={0}, use_global_device_ids=true | all-gather | bytes 6336 | tf_op jit(solution)/shard_map/all_gather | solution.py:123
  145.0 65.9 %all-gather.2 = f32[32,24,2]{1,2,0:T(2,128)S(1)} all-gather(f32[1,24,2]{1,2,0:T(2,128)} %bitcast.129), channel_id=1, replica_groups=mesh['dp'=8,'tensor'=4] {'dp','tensor'}, dimensions={0}, use_global_device_ids=true | all-gather | bytes 6336 | tf_op jit(solution)/shard_map/all_gather | solution.py:124
  213.0 8.6 %all_gather.48 = bf16[192,768]{0,1:T(8,128)(2,1)S(1)} all-gather(bf16[192,96]{0,1:T(8,128)(2,1)S(1)} %copy.41), channel_id=1, replica_groups=mesh['dp'=8,'tensor'=4] {'dp'}, dimensions={1}, use_global_device_ids=true | all-gather | bytes 331776 | tf_op jit(solution)/shard_map/all_gather | solution.py:132
  221.7 17.8 %all_gather.45 = bf16[512,768]{1,0:T(8,128)(2,1)S(1)} all-gather(bf16[128,768]{1,0:T(8,128)(2,1)S(1)} %fusion.21), channel_id=1, replica_groups=mesh['dp'=8,'tensor'=4] {'tensor'}, dimensions={0}, use_global_device_ids=true | all-gather | bytes 983040 | tf_op jit(solution)/shard_map/all_gather | solution.py:141
  239.5 11.2 %all_gather.46 = bf16[3,768,192]{2,1,0:T(8,128)(2,1)S(1)} all-gather(bf16[3,96,192]{2,1,0:T(8,128)(2,1)S(1)} %copy-done.29), channel_id=1, replica_groups=mesh['dp'=8,'tensor'=4] {'dp'}, dimensions={1}, use_global_device_ids=true | all-gather | bytes 995328 | tf_op jit(solution)/shard_map/all_gather | solution.py:131
  258.3 40.6 %all-reduce = f32[3072]{0:T(1024)S(1)} all-reduce(f32[3072]{0:T(1024)S(1)} %dynamic-update-slice), channel_id=1, replica_groups=mesh['dp'=8,'tensor'=4] {'dp','tensor'}, use_global_device_ids=true, to_apply=%add | all-reduce | flops 3072 | bytes 24576
  298.9 65.7 %all-gather.3 = f32[32,24,2]{1,2,0:T(2,128)S(1)} all-gather(f32[1,24,2]{1,2,0:T(2,128)S(1)} %bitcast.130), channel_id=1, replica_groups=mesh['dp'=8,'tensor'=4] {'dp','tensor'}, dimensions={0}, use_global_device_ids=true | all-gather | bytes 6336 | tf_op jit(solution)/shard_map/all_gather | solution.py:125
  366.1 17.3 %all_gather.54 = bf16[512,768]{1,0:T(8,128)(2,1)} all-gather(bf16[128,768]{1,0:T(8,128)(2,1)S(1)} %copy-done.20), channel_id=1, replica_groups=mesh['dp'=8,'tensor'=4] {'tensor'}, dimensions={0}, use_global_device_ids=true | all-gather | bytes 983040 | tf_op jit(solution)/shard_map/all_gather | solution.py:142
  385.9 17.7 %all_gather.50 = bf16[512,768]{1,0:T(8,128)(2,1)} all-gather(bf16[128,768]{1,0:T(8,128)(2,1)S(1)} %add_convert_fusion.1), channel_id=1, replica_groups=mesh['dp'=8,'tensor'=4] {'tensor'}, dimensions={0}, use_global_device_ids=true | all-gather | bytes 983040 | tf_op jit(solution)/shard_map/all_gather | solution.py:171
  403.6 3.4 convolution_add_fusion
  407.0 4.1 fusion.46
  412.0 2.0 fusion.32
  414.3 4.0 fusion.39
  418.3 29.7 %reduce-scatter.21.cloned.1.call-done = f32[128,768]{1,0:T(8,128)} async-done(((f32[512,768]{1,0:T(8,128)}), f32[128,768]{1,0:T(8,128)}) %reduce-scatter.21.cloned.1.call-update) | async-done | bytes 393232 | tf_op jit(solution)/shard_map/reduce_scatter | solution.py:197
  448.0 1.8 multiply_reduce_fusion.1
  450.4 34.2 %reduce-scatter.19.cloned.1.call-done = f32[128,768]{1,0:T(8,128)} async-done(((f32[512,768]{1,0:T(8,128)}), f32[128,768]{1,0:T(8,128)}) %reduce-scatter.19.cloned.1.call-update) | async-done | bytes 393232 | tf_op jit(solution)/shard_map/reduce_scatter | solution.py:176
  484.6 2.8 fusion.40
  488.2 18.2 %all_gather.55 = bf16[512,768]{1,0:T(8,128)(2,1)S(1)} all-gather(bf16[128,768]{1,0:T(8,128)(2,1)S(1)} %convert_element_type.70), channel_id=1, replica_groups=mesh['dp'=8,'tensor'=4] {'tensor'}, dimensions={0}, use_global_device_ids=true | all-gather | bytes 983040 | tf_op jit(solution)/shard_map/all_gather | solution.py:206
  508.9 2.2 multiply_reduce_fusion
  515.2 1.8 convolution_bitcast_fusion
  517.1 3.0 copy.55
  520.1 2.8 reshape.157
  524.3 2.0 convolution_bitcast_fusion.1
  527.4 2.4 fusion.38
  531.2 2.2 fusion.30
  534.7 8.6 %reduce-scatter.31.cloned.1.call-done = f32[96,192]{1,0:T(8,128)} async-done(((f32[768,192]{1,0:T(8,128)}), f32[96,192]{1,0:T(8,128)}) %reduce-scatter.31.cloned.1.call-update) | async-done | bytes 73744
  544.9 42.0 %reduce-scatter.29.cloned.1.call-done = f32[96,576]{1,0:T(8,128)} async-done(((f32[768,576]{1,0:T(8,128)}), f32[96,576]{1,0:T(8,128)}) %reduce-scatter.29.cloned.1.call-update) | async-done | bytes 221200
  588.8 35.8 %reduce-scatter.23.cloned.1.call-done = f32[128,768]{1,0:T(8,128)} async-done(((f32[512,768]{1,0:T(8,128)}), f32[128,768]{1,0:T(8,128)}) %reduce-scatter.23.cloned.1.call-update) | async-done | bytes 393232 | tf_op jit(solution)/shard_map/reduce_scatter | solution.py:221
  625.9 39.9 %all-reduce.6 = (f32[2,768]{1,0:T(2,128)S(1)}, f32[2,768]{1,0:T(2,128)S(1)}, f32[2,768]{1,0:T(2,128)S(1)}, f32[2,768]{1,0:T(2,128)S(1)}, f32[3072]{0:T(1024)S(1)}) all-reduce(f32[2,768]{1,0:T(2,128)S(1)} %pad_maximum_fusion.3, f32[2,768]{1,0:T(2,128)S(1)} %pad_maximum_fusion.4, ...), channel_id=6, replica_groups=mesh['dp'=8,'tensor'=4] {'dp','tensor'}, use_global_device_ids=true, to_apply=%region_17.18.clone | all-reduce | flops 9216 | bytes 73728
  668.9 1.9 fusion.26
  670.8 45.6 %reduce-scatter.25.cloned.1.call-done = f32[96,768]{1,0:T(8,128)} async-done(((f32[768,768]{1,0:T(8,128)}), f32[96,768]{1,0:T(8,128)}) %reduce-scatter.25.cloned.1.call-update) | async-done | bytes 294928 | tf_op jit(solution)/shard_map/reduce_scatter | solution.py:238
  (189 shorter events, 38.6 us)
Async XLA Ops:
  8.0 213.5 %copy-start.2 = (bf16[128,768]{1,0:T(8,128)(2,1)S(1)}, bf16[128,768]{1,0:T(8,128)(2,1)}, u32[]{:S(2)}) copy-start(bf16[128,768]{1,0:T(8,128)(2,1)} %param.12) | copy-start | bytes 589828
  8.0 231.5 %copy-start.29 = (bf16[3,96,192]{2,1,0:T(8,128)(2,1)S(1)}, bf16[3,96,192]{2,1,0:T(8,128)(2,1)}, u32[]{:S(2)}) copy-start(bf16[3,96,192]{2,1,0:T(8,128)(2,1)} %param.15) | copy-start | bytes 331780
  8.0 375.3 %reduce-scatter.17.cloned.1.call-start = ((), (), s32[]{:S(2)}) async-start(), calls=%async_computation.8 | async-start | bytes 1966080 | tf_op jit(solution)/shard_map/reduce_scatter | solution.py:160
  9.2 241.5 %copy-start.34 = (f32[128]{0:T(128)}, f32[128]{0:T(128)S(1)}, u32[]{:S(2)}) copy-start(f32[128]{0:T(128)S(1)} %broadcast_multiply_fusion.5) | copy-start | bytes 1540
  10.4 240.3 %copy-start.37 = (f32[128]{0:T(128)}, f32[128]{0:T(128)S(1)}, u32[]{:S(2)}) copy-start(f32[128]{0:T(128)S(1)} %add_rsqrt_fusion.1) | copy-start | bytes 1540
  212.9 40.6 %copy-start.4 = (pred[512,512]{0,1:T(8,128)(4,1)}, pred[512,512]{0,1:T(8,128)(4,1)S(1)}, u32[]{:S(2)}) copy-start(pred[512,512]{0,1:T(8,128)(4,1)S(1)} %fusion.12) | copy-start | bytes 786436
  221.5 33.0 %copy-start.11 = (bf16[192,768]{0,1:T(8,128)(2,1)}, bf16[192,768]{0,1:T(8,128)(2,1)S(1)}, u32[]{:S(2)}) copy-start(bf16[192,768]{0,1:T(8,128)(2,1)S(1)} %all_gather.48) | copy-start | bytes 884740
  239.5 12.1 %copy-start = (bf16[512,768]{1,0:T(8,128)(2,1)}, bf16[512,768]{1,0:T(8,128)(2,1)S(1)}, u32[]{:S(2)}) copy-start(bf16[512,768]{1,0:T(8,128)(2,1)S(1)} %all_gather.45) | copy-start | bytes 2359300
  251.1 1.7 copy-start.13
  252.0 1.5 copy-start.23
  255.2 2.8 copy-start.43
  255.2 43.7 %copy-start.41 = (f32[2,24]{1,0:T(2,128)S(1)}, f32[2,24]{1,0:T(2,128)}, u32[]{:S(2)}) copy-start(f32[2,24]{1,0:T(2,128)} %param.18) | copy-start | bytes 580
  256.8 109.3 %copy-start.20 = (bf16[128,768]{1,0:T(8,128)(2,1)S(1)}, bf16[128,768]{1,0:T(8,128)(2,1)}, u32[]{:S(2)}) copy-start(bf16[128,768]{1,0:T(8,128)(2,1)} %param.23) | copy-start | bytes 589828
  256.8 146.8 %all-gather.7.cloned.1.call-start = ((), (), s32[]{:S(2)}) async-start(), calls=%async_computation.9 | async-start | bytes 1327104 | tf_op jit(solution)/shard_map/all_gather | solution.py:133
  257.4 149.7 %all-gather.9.cloned.1.call-start = ((), (), s32[]{:S(2)}) async-start(), calls=%async_computation.10 | async-start | bytes 1327104 | tf_op jit(solution)/shard_map/all_gather | solution.py:134
  258.0 190.1 %reduce-scatter.21.cloned.1.call-start = ((), (), s32[]{:S(2)}) async-start(), calls=%async_computation.12 | async-start | bytes 1966080 | tf_op jit(solution)/shard_map/reduce_scatter | solution.py:197
  407.0 5.0 copy-start.42
  414.0 70.6 %reduce-scatter.19.cloned.1.call-start = ((), (), s32[]{:S(2)}) async-start(), calls=%async_computation.11 | async-start | bytes 1966080 | tf_op jit(solution)/shard_map/reduce_scatter | solution.py:176
  418.3 125.0 %reduce-scatter.31.cloned.1.call-start = ((), (), s32[]{:S(2)}) async-start(), calls=%async_computation.17 | async-start | bytes 884736
  484.6 21.7 %copy-start.12 = (bf16[192,768]{0,1:T(8,128)(2,1)S(1)}, bf16[192,768]{0,1:T(8,128)(2,1)}, u32[]{:S(2)}) copy-start(bf16[192,768]{0,1:T(8,128)(2,1)} %copy-done.11) | copy-start | bytes 884740
  487.5 20.0 %copy-start.18 = (bf16[3,64,512]{2,1,0:T(8,128)(2,1)S(1)}, bf16[3,64,512]{2,1,0:T(8,128)(2,1)}, u32[]{:S(2)}) copy-start(bf16[3,64,512]{2,1,0:T(8,128)(2,1)} %copy-done.17) | copy-start | bytes 589828
  508.8 78.1 %reduce-scatter.29.cloned.1.call-start = ((), (), s32[]{:S(2)}) async-start(), calls=%async_computation.16 | async-start | bytes 2211840
  513.0 1.5 copy-start.27
  513.5 1.7 copy-start.1
  522.9 101.7 %reduce-scatter.23.cloned.1.call-start = ((), (), s32[]{:S(2)}) async-start(), calls=%async_computation.13 | async-start | bytes 1966080 | tf_op jit(solution)/shard_map/reduce_scatter | solution.py:221
  524.3 2.1 copy-start.46
  526.3 144.5 %reduce-scatter.27.cloned.1.call-start = ((), (), s32[]{:S(2)}) async-start(), calls=%async_computation.15 | async-start | bytes 2654208 | tf_op jit(solution)/shard_map/reduce_scatter | solution.py:239
  529.8 186.6 %reduce-scatter.25.cloned.1.call-start = ((), (), s32[]{:S(2)}) async-start(), calls=%async_computation.14 | async-start | bytes 2654208 | tf_op jit(solution)/shard_map/reduce_scatter | solution.py:238
  533.4 91.2 %copy-start.3 = (bf16[128,768]{1,0:T(8,128)(2,1)S(1)}, bf16[128,768]{1,0:T(8,128)(2,1)}, u32[]{:S(2)}) copy-start(bf16[128,768]{1,0:T(8,128)(2,1)} %param.12) | copy-start | bytes 589828
  533.4 91.2 %copy-start.35 = (f32[128]{0:T(128)S(1)}, f32[128]{0:T(128)}, u32[]{:S(2)}) copy-start(f32[128]{0:T(128)} %copy-done.34) | copy-start | bytes 1540
  533.4 91.2 %copy-start.38 = (f32[128]{0:T(128)S(1)}, f32[128]{0:T(128)}, u32[]{:S(2)}) copy-start(f32[128]{0:T(128)} %copy-done.37) | copy-start | bytes 1540
  533.5 135.5 %copy-start.10 = (f32[128,768]{1,0:T(8,128)S(1)}, f32[128,768]{1,0:T(8,128)}, u32[]{:S(2)}) copy-start(f32[128,768]{1,0:T(8,128)} %copy-done.9) | copy-start | bytes 1179652
  (25 other events, 26.0 us)
Sparse Core Ops, SparseCore 0:
  256.9 35.1 reduce-scatter.16
  414.2 33.8 reduce-scatter.20
  450.4 34.2 reduce-scatter.18
Sparse Core Ops, SparseCore 1:
  259.2 22.7 all-gather.6
  283.7 24.2 all-gather.8
  508.9 34.3 reduce-scatter.30
  546.7 40.1 reduce-scatter.28
  589.3 35.2 reduce-scatter.22
  628.9 41.3 reduce-scatter.26
  674.1 42.3 reduce-scatter.24
where the time goes:
time: 725 us; the launch traced here: 724 us
  blocking collectives  437 us (60%)
  waiting for transfers between devices  197 us (27%)
  matrix products  33.2 us (5%)
  local copies, waits for them, and re-layouts  24.4 us (3%)
  between operations  15.9 us (2%)
  other arithmetic  15.6 us (2%)
    unnamed x2, blocking collectives  80.5 us
    all_gather x1, blocking collectives, shards(): lax.all_gather(norm_gain_pair, ('dp', 'tensor'), axis=1, tiled=True)  70 us
    all_gather x1, blocking collectives, shards(): lax.all_gather(qv_bias, ('dp', 'tensor'), axis=1, tiled=True)  65.9 us
    all_gather x1, blocking collectives, shards(): lax.all_gather(res_bias, ('dp', 'tensor'), axis=1, tiled=True)  65.7 us
    all_gather x1, blocking collectives, shards(): lax.all_gather(norm_bias_pair, ('dp', 'tensor'), axis=1, tiled=True)  63.8 us
    unnamed x12, waiting for transfers between devices  51.8 us
    reduce_scatter x1, waiting for transfers between devices, shards(): lax.psum_scatter(fc_grad, 'dp', scatter_dimension=0, tiled=True)  45.6 us
    reduce_scatter x1, waiting for transfers between devices, shards(): lax.psum_scatter(jnp.einsum('itw,idw->td', d_qkv, qkv_full, preferred_ele...  35.8 us
  transfers between devices with their start and end apart: 10, of which 6 were waited for; matrix products, arithmetic and copies ran while one was open for 6% of the time, Pallas kernels for 0%

commit v1 on v0

v1 whole, which is shorter than its diff:
```python
import functools

import jax
import jax.numpy as jnp
from jax import lax
from jax.experimental import pallas as pl
from jax.experimental.pallas import tpu as pltpu
from jax.sharding import PartitionSpec as P

HEAD_DIM = 64


epsilon = 1e-05
gelu_coeff = 0.044715
gelu_root = 0.7978845608028654


def layer_normalize(rows, norm_gain, norm_shift):
    centered_input = rows - jnp.mean(rows, axis=-1, keepdims=True)
    inverse_deviation = lax.rsqrt(
        jnp.mean(centered_input * centered_input, axis=-1, keepdims=True) + epsilon
    )
    standardized_input = centered_input * inverse_deviation
    return (standardized_input * norm_gain + norm_shift, standardized_input, inverse_deviation)


def layer_normalize_backward(output_gradient, standardized_input, inverse_deviation, norm_gain):
    scaled_rows = output_gradient * norm_gain
    return inverse_deviation * (
        scaled_rows
        - jnp.mean(scaled_rows, axis=-1, keepdims=True)
        - standardized_input * jnp.mean(scaled_rows * standardized_input, axis=-1, keepdims=True)
    )


def gelu_value(pre):
    return 0.5 * pre * (1.0 + jnp.tanh(gelu_root * (pre + gelu_coeff * pre * pre * pre)))


def gelu_slope(pre):
    tangent = jnp.tanh(gelu_root * (pre + gelu_coeff * pre * pre * pre))
    return 0.5 * (1.0 + tangent) + 0.5 * pre * (1.0 - tangent * tangent) * gelu_root * (
        1.0 + 3.0 * gelu_coeff * pre * pre
    )


def allowed_pairs(segment):
    length = segment.shape[0]
    rows = lax.broadcasted_iota(jnp.int32, (length, length), 0)
    cols = lax.broadcasted_iota(jnp.int32, (length, length), 1)
    return (segment[:, None] == segment[None, :]) & (rows >= cols)


def masked_scores(query, key, segment):
    scores = jnp.einsum(
        "qhd,khd->hqk", query, key, preferred_element_type=jnp.float32
    ) * HEAD_DIM ** (-0.5)
    return jnp.where(allowed_pairs(segment)[None], scores, -1e30)


def attend(pieces):
    query, key, value, segment = pieces
    scores = masked_scores(query, key, segment)
    peak = jnp.max(scores, axis=-1, keepdims=True)
    logsum = peak + jnp.log(jnp.sum(jnp.exp(scores - peak), axis=-1, keepdims=True))
    weights = jnp.exp(scores - logsum).astype(jnp.bfloat16)
    context = jnp.einsum("hqk,khd->qhd", weights, value, preferred_element_type=jnp.float32)
    return (context.astype(jnp.bfloat16), logsum)


def attend_back(pieces):
    query, key, value, segment, logsum, grad_context = pieces
    probs = jnp.exp(masked_scores(query, key, segment) - logsum)
    probs_half = probs.astype(jnp.bfloat16)
    grad_value = jnp.einsum(
        "hqk,qhd->khd", probs_half, grad_context, preferred_element_type=jnp.float32
    )
    grad_probs = jnp.einsum("qhd,khd->hqk", grad_context, value, preferred_element_type=jnp.float32)
    inner = jnp.sum(probs * grad_probs, axis=-1, keepdims=True)
    grad_scores = (probs * (grad_probs - inner)).astype(jnp.bfloat16)
    grad_query = jnp.einsum(
        "hqk,khd->qhd", grad_scores, key, preferred_element_type=jnp.float32
    ) * HEAD_DIM ** (-0.5)
    grad_key = jnp.einsum(
        "hqk,qhd->khd", grad_scores, query, preferred_element_type=jnp.float32
    ) * HEAD_DIM ** (-0.5)
    return (grad_query, grad_key, grad_value)


def contract_rows(left, right):
    return lax.dot_general(
        left, right, (((0,), (0,)), ((), ())), preferred_element_type=jnp.float32
    )


def contract_cols(left, right):
    return lax.dot_general(
        left, right, (((1,), (1,)), ((), ())), preferred_element_type=jnp.float32
    )


MESH = pl.DeviceIdType.MESH


def loop(count, body):
    if count <= 8:
        for step in range(count):
            body(step)
    else:

        def wrapped(step, carry):
            body(step)
            return carry

        lax.fori_loop(0, count, wrapped, 0)


def remote(src, dst, send, recv, device):
    return pltpu.make_async_remote_copy(
        src_ref=src, dst_ref=dst, send_sem=send, recv_sem=recv, device_id=device, device_id_type=MESH
    )


class FlatGather:
    def __init__(self, n, me, device, src, out, sems, local_sem):
        self.n, self.me, self.device, self.src, self.out, self.sems = n, me, device, src, out, sems
        self.local = pltpu.make_async_copy(src, out.at[me], local_sem)

    def copy(self, step):
        k = step + 1
        return remote(
            self.src,
            self.out.at[self.me],
            self.sems.at[0, k],
            self.sems.at[1, k],
            self.device(lax.rem(self.me + k, self.n)),
        )

    def start(self):
        loop(self.n - 1, lambda step: self.copy(step).start())
        self.local.start()

    def middle(self):
        pass

    def finish(self):
        loop(self.n - 1, lambda step: self.copy(step).wait())
        self.local.wait()


class PairGather:
    def __init__(self, n, me, device, src, out, sems, local_sem):
        self.n, self.me, self.device, self.src, self.out, self.sems = n, me, device, src, out, sems
        self.chips, self.core = n // 2, lax.rem(me, 2)
        self.chip = me // 2
        self.sibling = self.chip * 2 + 1 - self.core
        self.local = pltpu.make_async_copy(src, out.at[me], local_sem)

    def across(self, step):
        k = step + 1
        peer = lax.rem(self.chip + k, self.chips) * 2 + self.core
        return remote(
            self.src,
            self.out.at[self.me],
            self.sems.at[0, k],
            self.sems.at[1, k],
            self.device(peer),
        )

    def to_sibling(self):
        return remote(
            self.src,
            self.out.at[self.me],
            self.sems.at[0, 0],
            self.sems.at[1, 0],
            self.device(self.sibling),
        )

    def hand(self, step):
        k = step + 1
        slot = lax.rem(self.chip + self.chips - k, self.chips) * 2 + self.core
        return remote(
            self.out.at[slot],
            self.out.at[slot],
            self.sems.at[2, k],
            self.sems.at[3, k],
            self.device(self.sibling),
        )

    def start(self):
        loop(self.chips - 1, lambda step: self.across(step).start())
        self.to_sibling().start()
        self.local.start()

    def middle(self):
        def step_through(step):
            self.across(step).wait_recv()
            self.hand(step).start()

        loop(self.chips - 1, step_through)

    def finish(self):
        loop(self.chips - 1, lambda step: self.across(step).wait_send())
        self.to_sibling().wait()
        loop(self.chips - 1, lambda step: self.hand(step).wait())
        self.local.wait()


class FlatSum:
    def __init__(self, n, me, device, src, out, sems, slots):
        self.n, self.me, self.device, self.src, self.out, self.sems = n, me, device, src, out, sems
        self.slots = slots

    def copy(self, step):
        k = step + 1
        peer = lax.rem(self.me + k, self.n)
        return remote(
            self.src.at[peer],
            self.slots.at[k],
            self.sems.at[0, k],
            self.sems.at[1, k],
            self.device(peer),
        )

    def start(self):
        loop(self.n - 1, lambda step: self.copy(step).start())

    def middle(self):
        pass

    def finish(self):
        self.out[...] = self.src[self.me].astype(jnp.float32)

        def add(step):
            self.copy(step).wait()
            self.out[...] += self.slots[step + 1].astype(jnp.float32)

        loop(self.n - 1, add)


class PairSum:
    def __init__(self, n, me, device, src, out, sems, slots, sums):
        self.n, self.me, self.device, self.src, self.out, self.sems = n, me, device, src, out, sems
        self.slots, self.sums = slots, sums
        self.chips, self.core = n // 2, lax.rem(me, 2)
        self.chip = me // 2
        self.sibling = self.chip * 2 + 1 - self.core

    def trade(self, step):
        target = lax.rem(self.chip + step + 1, self.chips)
        return remote(
            self.src.at[target * 2 + 1 - self.core],
            self.slots.at[step],
            self.sems.at[0, step],
            self.sems.at[1, step],
            self.device(self.sibling),
        )

    def across(self, step):
        target = lax.rem(self.chip + step + 1, self.chips)
        return remote(
            self.sums.at[step],
            self.slots.at[self.chips + step],
            self.sems.at[2, step],
            self.sems.at[3, step],
            self.device(target * 2 + self.core),
        )

    def start(self):
        loop(self.chips, lambda step: self.trade(step).start())

    def middle(self):
        def pair(step):
            target = lax.rem(self.chip + step + 1, self.chips)
            self.trade(step).wait_recv()
            return self.src[target * 2 + self.core].astype(jnp.float32) + self.slots[step].astype(
                jnp.float32
            )

        def forward(step):
            self.sums[step] = pair(step).astype(self.sums.dtype)
            self.across(step).start()

        loop(self.chips - 1, forward)
        self.out[...] = pair(self.chips - 1)

    def finish(self):
        loop(self.chips, lambda step: self.trade(step).wait_send())

        def add(step):
            self.across(step).wait()
            self.out[...] += self.slots[self.chips + step].astype(jnp.float32)

        loop(self.chips - 1, add)


def exchange(dp, tensor, identity, ops):
    sizes = {"dp": dp, "tensor": tensor, "all": dp * tensor}
    arrays = [array for _, _, array in ops]
    outs, scratch, counts = [], [], []
    for form, axis, array in ops:
        n = sizes[axis]
        mine = [pltpu.SemaphoreType.DMA((4, n))]
        if form in (FlatGather, PairGather):
            outs.append(jax.ShapeDtypeStruct((n,) + array.shape, array.dtype))
            mine.append(pltpu.SemaphoreType.DMA)
        else:
            outs.append(jax.ShapeDtypeStruct(array.shape[1:], jnp.float32))
            mine.append(pltpu.VMEM(array.shape, array.dtype))
            if form is PairSum:
                mine.append(pltpu.VMEM((n // 2,) + array.shape[1:], array.dtype))
        scratch += mine
        counts.append(len(mine))
    axes = {axis for _, axis, _ in ops}

    def kernel(*refs):
        sources = refs[: len(ops)]
        results = refs[len(ops) : 2 * len(ops)]
        rest = list(refs[2 * len(ops) :])
        d, t = lax.axis_index("dp"), lax.axis_index("tensor")
        ranks = {"dp": d, "tensor": t, "all": d * tensor + t}
        devices = {
            "dp": lambda i: {"dp": i, "tensor": t},
            "tensor": lambda i: {"dp": d, "tensor": i},
            "all": lambda i: {"dp": i // tensor, "tensor": lax.rem(i, tensor)},
        }
        barrier = pltpu.get_barrier_semaphore()
        for axis in ["all"] if "all" in axes else sorted(axes):
            n = sizes[axis]

            def greet(step, n=n, axis=axis):
                pl.semaphore_signal(
                    barrier,
                    inc=1,
                    device_id=devices[axis](lax.rem(ranks[axis] + step + 1, n)),
                    device_id_type=MESH,
                )

            loop(n - 1, greet)
        pl.semaphore_wait(
            barrier,
            sizes["all"] - 1 if "all" in axes else sum(sizes[axis] - 1 for axis in axes),
        )
        work = []
        for (form, axis, _), src, out, count in zip(ops, sources, results, counts):
            work.append(form(sizes[axis], ranks[axis], devices[axis], src, out, *rest[:count]))
            del rest[:count]
        for op in work:
            op.start()
        for op in work:
            op.middle()
        for op in work:
            op.finish()

    return pl.pallas_call(
        kernel,
        out_shape=tuple(outs),
        in_specs=[pl.BlockSpec(memory_space=pltpu.VMEM)] * len(ops),
        out_specs=tuple([pl.BlockSpec(memory_space=pltpu.VMEM)] * len(ops)),
        scratch_shapes=scratch,
        compiler_params=pltpu.CompilerParams(
            collective_id=identity, has_side_effects=True, vmem_limit_bytes=40 * 2**20
        ),
        name="exchange_%d" % identity,
    )(*arrays)


def pad_to(array, axis, size):
    widths = [(0, 0)] * array.ndim
    widths[axis] = (0, size - array.shape[axis])
    return jnp.pad(array, widths) if size > array.shape[axis] else array


def standardize(rows):
    centered = rows - jnp.mean(rows, axis=-1, keepdims=True)
    inverse = lax.rsqrt(jnp.mean(centered * centered, axis=-1, keepdims=True) + epsilon)
    return centered * inverse, inverse


def shards(
    dp,
    tensor,
    tokens,
    norm_gain_pair,
    norm_bias_pair,
    w_qkv,
    qv_bias,
    w_out,
    res_bias,
    w_fc,
    fc_bias,
    w_proj,
    segments,
    cotangent,
):
    place = lax.axis_index("tensor")
    devices = dp * tensor
    width = tokens.shape[1]
    rows_own = w_qkv.shape[1]
    rows_pad = -(-rows_own // 16) * 16
    local_width = w_qkv.shape[2]
    local_hidden = w_fc.shape[1]
    seqs, length = segments.shape
    heads_local = local_width // HEAD_DIM
    head_start = place * local_width
    hidden_start = place * local_hidden
    small = norm_gain_pair.shape[1]
    fc_rows = fc_bias.shape[0] // small
    half = jnp.bfloat16

    attention_weights = jnp.concatenate([w_qkv[0], w_qkv[1], w_qkv[2], w_out.T], axis=1)
    tiny = jnp.concatenate(
        [norm_gain_pair, norm_bias_pair, qv_bias, res_bias, fc_bias.reshape(fc_rows, small)], axis=0
    )
    tiny = pad_to(pad_to(tiny, 1, 128), 0, 16)
    tokens_all, cot_all, w_attn, w_fc_all, w_proj_all, tiny_all = exchange(
        dp,
        tensor,
        1,
        [
            (FlatGather, "tensor", tokens),
            (FlatGather, "tensor", cotangent),
            (PairGather, "dp", pad_to(attention_weights, 0, rows_pad)),
            (PairGather, "dp", pad_to(w_fc, 0, rows_pad)),
            (PairGather, "dp", pad_to(w_proj.T, 0, rows_pad)),
            (FlatGather, "all", tiny),
        ],
    )
    rows_all = tokens.shape[0] * tensor
    tokens_all = tokens_all.reshape(rows_all, width)
    cot_all = cot_all.reshape(rows_all, width)
    w_attn = w_attn[:, :rows_own].reshape(width, 4 * local_width)
    w_fc_all = w_fc_all[:, :rows_own].reshape(width, local_hidden)
    w_proj_all = w_proj_all[:, :rows_own].reshape(width, local_hidden)
    w_in, w_out_t = w_attn[:, : 3 * local_width], w_attn[:, 3 * local_width :]
    vectors = tiny_all[:, :8, :small].transpose(1, 0, 2).reshape(8, width)
    norm_gains, norm_shifts, qv_whole, res_whole = (
        vectors[0:2],
        vectors[2:4],
        vectors[4:6],
        vectors[6:8],
    )
    qv_local = lax.dynamic_slice_in_dim(qv_whole, head_start, local_width, 1)
    fc_local = lax.dynamic_slice_in_dim(tiny_all, place * dp, dp, 0)[
        :, 8 : 8 + fc_rows, :small
    ].reshape(local_hidden)

    xhat1_all, _ = standardize(tokens_all.astype(jnp.float32))
    ln1_all = (xhat1_all * norm_gains[0] + norm_shifts[0]).astype(half)
    residual_stream = tokens.astype(jnp.float32)
    first_standardized, first_inverse_deviation = standardize(residual_stream)
    qkv = jnp.dot(ln1_all, w_in, preferred_element_type=jnp.float32)
    bias3 = jnp.concatenate([qv_local[0], jnp.zeros_like(qv_local[0]), qv_local[1]])
    qkv = (qkv + bias3).astype(half)

    def split(array):
        return array.reshape(seqs, length, heads_local, HEAD_DIM)

    query, keys, value = (
        split(qkv[:, i * local_width : (i + 1) * local_width]) for i in range(3)
    )
    context, logsum = lax.map(attend, (query, keys, value, segments))
    context = context.reshape(rows_all, local_width)
    attn_part = contract_cols(context, w_out_t).astype(half)
    (attn_sum,) = exchange(
        dp, tensor, 2, [(FlatSum, "tensor", attn_part.reshape(tensor, -1, width))]
    )
    first_hidden = residual_stream + attn_sum + res_whole[0]
    second_standardized, second_inverse_deviation = standardize(first_hidden)
    ln2 = (second_standardized * norm_gains[1] + norm_shifts[1]).astype(half)
    (ln2_all,) = exchange(dp, tensor, 3, [(FlatGather, "tensor", ln2)])
    ln2_all = ln2_all.reshape(rows_all, width)
    pre = jnp.dot(ln2_all, w_fc_all, preferred_element_type=jnp.float32) + fc_local
    act = gelu_value(pre).astype(half)
    mlp_part = contract_cols(act, w_proj_all).astype(half)
    d_pre = jnp.dot(cot_all, w_proj_all, preferred_element_type=jnp.float32) * gelu_slope(pre)
    fcb_grad = jnp.sum(d_pre, axis=0)
    d_pre_half = d_pre.astype(half)
    d_ln2_part = contract_cols(d_pre_half, w_fc_all).astype(half)
    proj_grad = contract_rows(cot_all, act).astype(half)
    fc_grad = contract_rows(ln2_all, d_pre_half).astype(half)

    def blocks(array):
        return pad_to(array.reshape(dp, rows_own, array.shape[1]), 1, rows_pad)

    d_ln2, mlp_sum, proj_part, fc_part = exchange(
        dp,
        tensor,
        4,
        [
            (FlatSum, "tensor", d_ln2_part.reshape(tensor, -1, width)),
            (FlatSum, "tensor", mlp_part.reshape(tensor, -1, width)),
            (PairSum, "dp", blocks(proj_grad)),
            (PairSum, "dp", blocks(fc_grad)),
        ],
    )
    block_out = (first_hidden + mlp_sum + res_whole[1]).astype(half)
    residual_gradient = cotangent.astype(jnp.float32)
    res1_grad = jnp.sum(residual_gradient, axis=0)
    second_gain_gradient = jnp.sum(d_ln2 * second_standardized, axis=0)
    shift2_grad = jnp.sum(d_ln2, axis=0)
    first_hidden_gradient = residual_gradient + layer_normalize_backward(
        d_ln2, second_standardized, second_inverse_deviation, norm_gains[1]
    )
    res0_grad = jnp.sum(first_hidden_gradient, axis=0)
    (d_hidden_all,) = exchange(
        dp, tensor, 5, [(FlatGather, "tensor", first_hidden_gradient.astype(half))]
    )
    d_hidden_all = d_hidden_all.reshape(rows_all, width)
    out_grad = contract_rows(d_hidden_all, context)
    d_context = jnp.dot(d_hidden_all, w_out_t, preferred_element_type=jnp.float32).astype(half)
    grads = lax.map(attend_back, (query, keys, value, segments, logsum, split(d_context)))
    grad_query, grad_key, grad_value = (grad.reshape(rows_all, local_width) for grad in grads)
    qb_grad = jnp.sum(grad_query, axis=0)
    vb_grad = jnp.sum(grad_value, axis=0)
    d_qkv = jnp.concatenate([grad_query, grad_key, grad_value], axis=1).astype(half)
    qkv_grad = contract_rows(ln1_all, d_qkv)
    attn_grad = jnp.concatenate([qkv_grad, out_grad], axis=1).astype(half)
    d_ln1_part = contract_cols(d_qkv, w_in)
    first_gain_gradient = jnp.sum(d_ln1_part * xhat1_all, axis=0)
    shift1_grad = jnp.sum(d_ln1_part, axis=0)

    qv_spread = lax.dynamic_update_slice(
        jnp.zeros((2, width), jnp.float32), jnp.stack([qb_grad, vb_grad]), (0, head_start)
    )
    fc_spread = lax.dynamic_update_slice(
        jnp.zeros((devices, fc_rows, small), jnp.float32),
        fcb_grad.reshape(dp, fc_rows, small),
        (place * dp, 0, 0),
    )
    vector_grads = jnp.stack(
        [
            first_gain_gradient,
            second_gain_gradient,
            shift1_grad,
            shift2_grad,
            qv_spread[0],
            qv_spread[1],
            res0_grad,
            res1_grad,
        ]
    )
    tiny_grads = jnp.concatenate(
        [vector_grads.reshape(8, devices, small).transpose(1, 0, 2), fc_spread], axis=1
    )
    tiny_grads = pad_to(pad_to(tiny_grads, 2, 128), 1, 16)
    d_ln1, attn_grad_part, tiny_sum = exchange(
        dp,
        tensor,
        6,
        [
            (FlatSum, "tensor", d_ln1_part.astype(half).reshape(tensor, -1, width)),
            (PairSum, "dp", blocks(attn_grad)),
            (FlatSum, "all", tiny_grads),
        ],
    )
    block_input_gradient = (
        first_hidden_gradient
        + layer_normalize_backward(
            d_ln1, first_standardized, first_inverse_deviation, norm_gains[0]
        )
    ).astype(half)
    attn_grad_part = attn_grad_part[:rows_own]
    qkv_part = jnp.stack(
        [attn_grad_part[:, i * local_width : (i + 1) * local_width] for i in range(3)]
    )
    return (
        block_out,
        block_input_gradient,
        tiny_sum[0:2, :small],
        tiny_sum[2:4, :small],
        qkv_part,
        tiny_sum[4:6, :small],
        attn_grad_part[:, 3 * local_width :].T,
        tiny_sum[6:8, :small],
        fc_part[:rows_own],
        tiny_sum[8 : 8 + fc_rows, :small].reshape(fc_bias.shape[0]),
        proj_part[:rows_own].T,
    )


def solution(mesh):
    return jax.shard_map(
        functools.partial(shards, mesh.shape["dp"], mesh.shape["tensor"]),
        mesh=mesh,
        in_specs=(
            P(("dp", "tensor"), None),
            P(None, ("dp", "tensor")),
            P(None, ("dp", "tensor")),
            P(None, "dp", "tensor"),
            P(None, ("dp", "tensor")),
            P("tensor", "dp"),
            P(None, ("dp", "tensor")),
            P("dp", "tensor"),
            P(("dp", "tensor")),
            P("tensor", "dp"),
            P("dp", None),
            P(("dp", "tensor"), None),
        ),
        out_specs=(
            P(("dp", "tensor"), None),
            P(("dp", "tensor"), None),
            P(None, ("dp", "tensor")),
            P(None, ("dp", "tensor")),
            P(None, "dp", "tensor"),
            P(None, ("dp", "tensor")),
            P("tensor", "dp"),
            P(None, ("dp", "tensor")),
            P("dp", "tensor"),
            P(("dp", "tensor")),
            P("tensor", "dp"),
        ),
        check_vma=False,
    )
```

time: 725 us -> 233 us (0.32)
  blocking collectives: 437 us -> 0 us
  waiting for transfers between devices: 197 us -> 0 us
  Pallas kernels: 0 us -> 178 us
  between operations: 15.9 us -> 1.7 us
  matrix products: 33.2 us -> 19.1 us
    all_gather x10 -> x0, blocking collectives: 356 us -> none  [the longest x1 70 us: shards(): lax.all_gather(norm_gain_pair, ('dp', 'tensor'), axis=1, tiled=True)]
    pallas_call x0 -> x6, Pallas kernels: none -> 178 us  [exchange(): pl.pallas_call(kernel, out_shape=tuple(outs), in_specs=[pl.BlockSpec(memo...]
    reduce_scatter x6 -> x0, waiting for transfers between devices: 145 us -> none  [the longest x1 45.6 us: shards(): lax.psum_scatter(fc_grad, 'dp', scatter_dimension=0, tiled=True)]
    unnamed x2 -> x0, blocking collectives: 80.5 us -> none
    unnamed x12 -> x0, waiting for transfers between devices: 51.8 us -> none
    unnamed x112 -> x124, local copies, waits for them, and re-layouts: 21.9 us -> 13.3 us
    dot_general x8 -> x4, matrix products: 14.1 us -> 5.45 us  [the longest x1 2.19 us: shards(): jnp.dot(ln2_all, w_fc_all, preferred_element_type=jnp.float32) + fc_local]
  transfers between devices with their start and end apart: 10 -> 0, of which waited for: 6 -> 0; matrix products, arithmetic and copies ran while one was open for 6% -> 0% of each run, Pallas kernels for 0% -> 0%
where the time goes in v1:
time: 233 us; the launch traced here: 232 us
  Pallas kernels  178 us (76%)
  local copies, waits for them, and re-layouts  22.6 us (10%)
  matrix products  19.1 us (8%)
  other arithmetic  10.4 us (4%)
    pallas_call x6, Pallas kernels, exchange(): pl.pallas_call(kernel, out_shape=tuple(outs), in_specs=[pl.BlockSpec(memo...  178 us
    unnamed x124, local copies, waits for them, and re-layouts  13.3 us

profile of v1, /device:TPU:0, one launch (start us, length us, event | category | flops | bytes accessed | tf_op | source)
XLA Modules:
  0.0 232.2 jit_solution(1127682251195081361)
XLA Ops:
  0.6 0.9 copy.31
  1.5 0.9 slice_bitcast_fusion.7
  4.0 0.9 copy-done
  4.9 0.9 copy-done.2
  5.9 0.9 copy-done.10
  6.8 0.9 copy-done.11
  7.7 50.1 %exchange_1.1 = (bf16[4,128,768]{2,1,0:T(8,128)(2,1)S(1)}, bf16[4,128,768]{2,1,0:T(8,128)(2,1)S(1)}, bf16[8,96,768]{2,1,0:T(8,128)(2,1)S(1)}, bf16[8,96,768]{2,1...) custom-call(bf16[128,768]{1,0:T(8,128)(2,1)S(1)} %copy-done, ...), custom_call_target="tpu_custom_call" | custom-call | tf_op jit(solution)/shard_map/exchange_1/pallas_call | solution.py:355
  57.8 1.0 copy-done.12
  58.9 1.0 copy-done.14
  59.9 0.9 copy-done.16
  60.8 0.9 slice_reduce_fusion
  65.9 0.9 copy-done.18
  66.8 1.0 convolution_convert_fusion.8
  68.5 17.4 %exchange_2.1 = f32[128,768]{1,0:T(8,128)S(1)} custom-call(bf16[4,128,768]{2,1,0:T(8,128)(2,1)S(1)} %bitcast.107), custom_call_target="tpu_custom_call" | custom-call | tf_op jit(solution)/shard_map/exchange_2/pallas_call | solution.py:355
  87.4 19.3 %exchange_3.1 = bf16[4,128,768]{2,1,0:T(8,128)(2,1)S(1)} custom-call(bf16[128,768]{1,0:T(8,128)(2,1)S(1)} %add_convert_fusion.2.refs_0_), custom_call_target="tpu_custom_call" | custom-call | tf_op jit(solution)/shard_map/exchange_3/pallas_call | solution.py:355
  106.8 2.2 convolution_add_fusion
  109.0 2.0 fusion.45
  111.9 1.1 convolution_convert_fusion.3
  113.0 0.9 convolution_convert_fusion.1
  114.8 39.2 %exchange_4.1 = (f32[128,768]{1,0:T(8,128)S(1)}, f32[128,768]{1,0:T(8,128)S(1)}, f32[96,768]{1,0:T(8,128)S(1)}, f32[96,768]{1,0:T(8,128)S(1)}) custom-call(bf16[4,128,768]{2,1,0:T(8,128)(2,1)S(1)} %bitcast.113, bf16[4,128,768]{2,1,0:T(8,128)(2,1)S(1)} %bitcast.114, bf16[8,96,768]{2,1,0:T(8,128)(2,1)S(1)} %bitcast.108, bf16[8,96,768]{2,1,0:T(8,128)(2,1)S(1)} %bitcast.109), custom_call_target="tpu_custom_call" | custom-call | tf_op jit(solution)/shard_map/exchange_4/pallas_call | solution.py:355
  157.2 1.4 add.167
  158.6 2.3 %fusion.38 = (f32[768]{0:T(1024)}, f32[128,768]{1,0:T(8,128)S(1)}, bf16[128,768]{1,0:T(8,128)(2,1)}, f32[768]{0:T(1024)}) fusion(f32[128]{0:T(128)} %broadcast_multiply_fusion.4, f32[128,768]{1,0:T(8,128)S(1)} %copy-done.21, f32[128]{0:T(128)} %copy-done.42, f32[128]{0:T(128)} %broadcast_multiply_fusion.5, f32[128,768]{1,0:T(8,128)S(1)} %get-tuple-element.82, ...), kind=kLoop, calls=%fused_computation.113 | loop fusion | flops 1374720 | bytes 1980416 | tf_op jit(solution)/shard_map/reduce_sum | solution.py:505
  161.0 18.9 %exchange_5.1 = bf16[4,128,768]{2,1,0:T(8,128)(2,1)S(1)} custom-call(bf16[128,768]{1,0:T(8,128)(2,1)S(1)} %convert_element_type.108.refs_0_), custom_call_target="tpu_custom_call" | custom-call | tf_op jit(solution)/shard_map/exchange_5/pallas_call | solution.py:355
  180.6 1.6 fusion.43
  182.2 1.2 multiply_reduce_fusion
  183.4 0.9 multiply_convert_fusion
  185.8 1.5 fusion.37
  187.3 1.2 copy.38
  188.5 1.6 convolution_convert_fusion.6
  190.3 0.8 convolution_convert_fusion.2
  193.3 33.5 %exchange_6.1 = (f32[128,768]{1,0:T(8,128)S(1)}, f32[96,768]{1,0:T(8,128)S(1)}, f32[16,128]{1,0:T(8,128)S(1)}) custom-call(bf16[4,128,768]{2,1,0:T(8,128)(2,1)S(1)} %bitcast.110, bf16[8,96,768]{2,1,0:T(8,128)(2,1)S(1)} %pad_maximum_fusion.refs_1_, f32[32,16,128]{2,1,0:T(8,128)S(1)} %pad.19.refs_2_), custom_call_target="tpu_custom_call" | custom-call | tf_op jit(solution)/shard_map/exchange_6/pallas_call | solution.py:355
  227.1 0.9 fusion.25
  (190 shorter events, 21.3 us)
Async XLA Ops:
  60.8 119.2 %copy-start.4 = (bf16[8,96,768]{2,1,0:T(8,128)(2,1)}, bf16[8,96,768]{2,1,0:T(8,128)(2,1)S(1)}, u32[]{:S(2)}) copy-start(bf16[8,96,768]{2,1,0:T(8,128)(2,1)S(1)} %get-tuple-element.77) | copy-start | bytes 3538948
  64.1 1.8 copy-start.34
  64.4 1.5 copy-start.22
  65.2 1.7 copy-start.18
  67.8 18.1 %copy-start.1 = (bf16[128,768]{1,0:T(8,128)(2,1)S(1)}, bf16[128,768]{1,0:T(8,128)(2,1)}, u32[]{:S(2)}) copy-start(bf16[128,768]{1,0:T(8,128)(2,1)} %refs_0_.1) | copy-start | bytes 589828
  87.0 22.0 %copy-start.42 = (f32[128]{0:T(128)}, f32[128]{0:T(128)S(1)}, u32[]{:S(2)}) copy-start(f32[128]{0:T(128)S(1)} %get-tuple-element.164) | copy-start | bytes 1540
  87.2 21.8 %copy-start.51 = (f32[128]{0:T(128)}, f32[128]{0:T(128)S(1)}, u32[]{:S(2)}) copy-start(f32[128]{0:T(128)S(1)} %add_rsqrt_fusion.1) | copy-start | bytes 1540
  106.8 2.2 copy-start.13
  106.8 2.2 copy-start.17
  109.0 2.1 copy-start.15
  114.8 40.7 %copy-start.21 = (f32[128,768]{1,0:T(8,128)S(1)}, f32[128,768]{1,0:T(8,128)}, u32[]{:S(2)}) copy-start(f32[128,768]{1,0:T(8,128)} %copy-done.20) | copy-start | bytes 1179652
  114.8 40.7 %copy-start.43 = (f32[128]{0:T(128)S(1)}, f32[128]{0:T(128)}, u32[]{:S(2)}) copy-start(f32[128]{0:T(128)} %copy-done.42) | copy-start | bytes 1540
  114.8 40.7 %copy-start.52 = (f32[128]{0:T(128)S(1)}, f32[128]{0:T(128)}, u32[]{:S(2)}) copy-start(f32[128]{0:T(128)} %copy-done.51) | copy-start | bytes 1540
  114.8 43.8 %copy-start.3 = (bf16[128,768]{1,0:T(8,128)(2,1)S(1)}, bf16[128,768]{1,0:T(8,128)(2,1)}, u32[]{:S(2)}) copy-start(bf16[128,768]{1,0:T(8,128)(2,1)} %refs_1_.1) | copy-start | bytes 589828
  158.6 21.9 %copy-start.19 = (f32[3,512,512]{1,2,0:T(8,128)S(1)}, f32[3,512,512]{1,2,0:T(8,128)}, u32[]{:S(2)}) copy-start(f32[3,512,512]{1,2,0:T(8,128)} %copy-done.18) | copy-start | bytes 9437188
  161.0 21.2 %copy-start.24 = (f32[128,768]{1,0:T(8,128)}, f32[128,768]{1,0:T(8,128)S(1)}, u32[]{:S(2)}) copy-start(f32[128,768]{1,0:T(8,128)S(1)} %get-tuple-element.125) | copy-start | bytes 1179652
  161.0 19.6 %copy-start.23 = (pred[512,512]{0,1:T(8,128)(4,1)S(1)}, pred[512,512]{0,1:T(8,128)(4,1)}, u32[]{:S(2)}) copy-start(pred[512,512]{0,1:T(8,128)(4,1)} %copy-done.22) | copy-start | bytes 786436
  180.5 1.6 copy-start.35
  182.2 3.5 %copy-start.58 = (bf16[512,3,64]{0,2,1:T(8,128)(2,1)}, bf16[512,3,64]{0,2,1:T(8,128)(2,1)S(1)}, u32[]{:S(2)}) copy-start(bf16[512,3,64]{0,2,1:T(8,128)(2,1)S(1)} %get-tuple-element.135) | copy-start | bytes 589828
  184.3 1.4 copy-start.5
  184.3 1.4 copy-start.46
  184.4 1.4 copy-start.48
  187.3 2.7 %copy-start.27 = (bf16[512,768]{1,0:T(8,128)(2,1)S(1)}, bf16[512,768]{1,0:T(8,128)(2,1)}, u32[]{:S(2)}) copy-start(bf16[512,768]{1,0:T(8,128)(2,1)} %copy-done.26) | copy-start | bytes 2359300
  188.4 1.9 copy-start.37
  188.5 1.9 copy-start.59
  191.2 1.6 copy-start.39
  191.2 1.7 copy-start.38
  193.2 33.6 %copy-start.50 = (f32[128]{0:T(128)S(1)}, f32[128]{0:T(128)}, u32[]{:S(2)}) copy-start(f32[128]{0:T(128)} %copy-done.49) | copy-start | bytes 1540
  193.2 33.6 %copy-start.53 = (f32[128]{0:T(128)S(1)}, f32[128]{0:T(128)}, u32[]{:S(2)}) copy-start(f32[128]{0:T(128)} %get-tuple-element.163) | copy-start | bytes 1540
  193.3 33.8 %copy-start.25 = (f32[128,768]{1,0:T(8,128)S(1)}, f32[128,768]{1,0:T(8,128)}, u32[]{:S(2)}) copy-start(f32[128,768]{1,0:T(8,128)} %copy-done.24) | copy-start | bytes 1179652
  226.8 3.9 %copy-start.9 = (f32[96,768]{1,0:T(8,128)S(1)}, f32[96,768]{1,0:T(8,128)}, u32[]{:S(2)}) copy-start(f32[96,768]{1,0:T(8,128)} %copy-done.8) | copy-start | bytes 884740
  227.1 4.4 %copy-start.7 = (f32[96,768]{1,0:T(8,128)S(1)}, f32[96,768]{1,0:T(8,128)}, u32[]{:S(2)}) copy-start(f32[96,768]{1,0:T(8,128)} %copy-done.6) | copy-start | bytes 884740
  (28 other events, 25.0 us)

commit v2 on v1

--- a/solution.py
+++ b/solution.py
@@ -121,31 +121,223 @@
     )
 
 
-class FlatGather:
+class GridGather:
+    def __init__(self, dp, tensor, d, t, src, out, sems, local_sem):
+        self.dp, self.tensor, self.d, self.t = dp, tensor, d, t
+        self.src, self.out, self.sems = src, out, sems
+        self.local = pltpu.make_async_copy(src, out.at[d, t], local_sem)
+
+    def first(self, step):
+        k = step + 1
+        return remote(
+            self.src,
+            self.out.at[self.d, self.t],
+            self.sems.at[0, k],
+            self.sems.at[1, k],
+            {"dp": self.d, "tensor": lax.rem(self.t + k, self.tensor)},
+        )
+
+    def second(self, step):
+        k = step + 1
+        return remote(
+            self.out.at[self.d],
+            self.out.at[self.d],
+            self.sems.at[2, k],
+            self.sems.at[3, k],
+            {"dp": lax.rem(self.d + k, self.dp), "tensor": self.t},
+        )
+
+    def start(self):
+        self.local.start()
+        loop(self.tensor - 1, lambda step: self.first(step).start())
+
+    def middle(self):
+        self.local.wait()
+        loop(self.tensor - 1, lambda step: self.first(step).wait())
+        loop(self.dp - 1, lambda step: self.second(step).start())
+
+    def finish(self):
+        loop(self.dp - 1, lambda step: self.second(step).wait())
+
+
+class GridSum:
+    def __init__(self, dp, tensor, d, t, src, out, sems, slots, sums):
+        self.dp, self.tensor, self.d, self.t = dp, tensor, d, t
+        self.src, self.out, self.sems = src, out, sems
+        self.slots, self.sums = slots, sums
+
+    def first(self, step):
+        k = step + 1
+        peer = lax.rem(self.d + k, self.dp)
+        return remote(
+            self.src.at[peer],
+            self.slots.at[k],
+            self.sems.at[0, k],
+            self.sems.at[1, k],
+            {"dp": peer, "tensor": self.t},
+        )
+
+    def second(self, step):
+        k = step + 1
+        peer = lax.rem(self.t + k, self.tensor)
+        return remote(
+            self.sums.at[0, peer],
+            self.sums.at[1, k],
+            self.sems.at[2, k],
+            self.sems.at[3, k],
+            {"dp": self.d, "tensor": peer},
+        )
+
+    def start(self):
+        loop(self.dp - 1, lambda step: self.first(step).start())
+
+    def middle(self):
+        self.sums[0] = self.src[self.d]
+
+        def add(step):
+            self.first(step).wait()
+            self.sums[0] += self.slots[step + 1]
+
+        loop(self.dp - 1, add)
+        loop(self.tensor - 1, lambda step: self.second(step).start())
+
+    def finish(self):
+        self.out[...] = self.sums[0, self.t]
+
+        def add(step):
+            self.second(step).wait()
+            self.out[...] += self.sums[1, step + 1]
+
+        loop(self.tensor - 1, add)
+
+
+class LineGather:
     def __init__(self, n, me, device, src, out, sems, local_sem):
         self.n, self.me, self.device, self.src, self.out, self.sems = n, me, device, src, out, sems
         self.local = pltpu.make_async_copy(src, out.at[me], local_sem)
 
-    def copy(self, step):
-        k = step + 1
-        return remote(
-            self.src,
-            self.out.at[self.me],
-            self.sems.at[0, k],
-            self.sems.at[1, k],
-            self.device(lax.rem(self.me + k, self.n)),
+    def move(self, side, block, src=None):
+        peer = lax.rem(self.me + (1 if side == 0 else self.n - 1), self.n)
+        return remote(
+            self.out.at[block] if src is None else src,
+            self.out.at[block],
+            self.sems.at[2 * side, block],
+            self.sems.at[2 * side + 1, block],
+            self.device(peer),
         )
 
     def start(self):
-        loop(self.n - 1, lambda step: self.copy(step).start())
+        @pl.when(self.me < self.n - 1)
+        def _():
+            self.move(0, self.me, self.src).start()
+
+        @pl.when(self.me > 0)
+        def _():
+            self.move(1, self.me, self.src).start()
+
         self.local.start()
 
     def middle(self):
-        pass
+        for step in range(1, self.n):
+
+            @pl.when(self.me >= step)
+            def _():
+                block = self.me - step
+                self.move(0, block).wait_recv()
+
+                @pl.when(self.me < self.n - 1)
+                def _():
+                    self.move(0, block).start()
+
+            @pl.when(self.me + step < self.n)
+            def _():
+                block = self.me + step
+                self.move(1, block).wait_recv()
+
+                @pl.when(self.me > 0)
+                def _():
+                    self.move(1, block).start()
 
     def finish(self):
-        loop(self.n - 1, lambda step: self.copy(step).wait())
+        for step in range(self.n):
+
+            @pl.when((self.me >= step) & (self.me < self.n - 1))
+            def _():
+                self.move(0, self.me - step).wait_send()
+
+            @pl.when((self.me + step < self.n) & (self.me > 0))
+            def _():
+                self.move(1, self.me + step).wait_send()
+
         self.local.wait()
+
+
+class LineSum:
+    def __init__(self, n, me, device, src, out, sems, slots):
+        self.n, self.me, self.device, self.src, self.out, self.sems = n, me, device, src, out, sems
+        self.slots = slots
+
+    def move(self, side, block, first=False):
+        peer = lax.rem(self.me + (1 if side == 0 else self.n - 1), self.n)
+        return remote(
+            self.src.at[block] if first else self.slots.at[side, block],
+            self.slots.at[side, block],
+            self.sems.at[2 * side, block],
+            self.sems.at[2 * side + 1, block],
+            self.device(peer),
+        )
+
+    def start(self):
+        @pl.when(self.me == 0)
+        def _():
+            for step in range(self.n - 1):
+                self.move(0, self.n - 1 - step, True).start()
+
+        @pl.when(self.me == self.n - 1)
+        def _():
+            for step in range(self.n - 1):
+                self.move(1, step, True).start()
+
+    def forward(self, side, block):
+        self.move(side, block).wait_recv()
+        self.slots[side, block] = (
+            self.slots[side, block].astype(jnp.float32) + self.src[block].astype(jnp.float32)
+        ).astype(self.slots.dtype)
+        self.move(side, block).start()
+
+    def middle(self):
+        for step in range(self.n - 1):
+
+            @pl.when((self.me > 0) & (self.me < self.n - 1 - step))
+            def _():
+                self.forward(0, self.n - 1 - step)
+
+            @pl.when((self.me < self.n - 1) & (self.me > step))
+            def _():
+                self.forward(1, step)
+
+    def finish(self):
+        self.out[...] = self.src[self.me].astype(jnp.float32)
+
+        @pl.when(self.me > 0)
+        def _():
+            self.move(0, self.me).wait_recv()
+            self.out[...] += self.slots[0, self.me].astype(jnp.float32)
+
+        @pl.when(self.me < self.n - 1)
+        def _():
+            self.move(1, self.me).wait_recv()
+            self.out[...] += self.slots[1, self.me].astype(jnp.float32)
+
+        for block in range(self.n):
+
+            @pl.when(self.me < block)
+            def _():
+                self.move(0, block).wait_send()
+
+            @pl.when(self.me > block)
+            def _():
+                self.move(1, block).wait_send()
 
 
 class PairGather:
@@ -206,38 +398,6 @@
         self.local.wait()
 
 
-class FlatSum:
-    def __init__(self, n, me, device, src, out, sems, slots):
-        self.n, self.me, self.device, self.src, self.out, self.sems = n, me, device, src, out, sems
-        self.slots = slots
-
-    def copy(self, step):
-        k = step + 1
-        peer = lax.rem(self.me + k, self.n)
-        return remote(
-            self.src.at[peer],
-            self.slots.at[k],
-            self.sems.at[0, k],
-            self.sems.at[1, k],
-            self.device(peer),
-        )
-
-    def start(self):
-        loop(self.n - 1, lambda step: self.copy(step).start())
-
-    def middle(self):
-        pass
-
-    def finish(self):
-        self.out[...] = self.src[self.me].astype(jnp.float32)
-
-        def add(step):
-            self.copy(step).wait()
-            self.out[...] += self.slots[step + 1].astype(jnp.float32)
-
-        loop(self.n - 1, add)
-
-
 class PairSum:
     def __init__(self, n, me, device, src, out, sems, slots, sums):
         self.n, self.me, self.device, self.src, self.out, self.sems = n, me, device, src, out, sems
@@ -300,32 +460,42 @@
     outs, scratch, counts = [], [], []
     for form, axis, array in ops:
         n = sizes[axis]
-        mine = [pltpu.SemaphoreType.DMA((4, n))]
-        if form in (FlatGather, PairGather):
+        mine = [pltpu.SemaphoreType.DMA((4, max(dp, tensor) if axis == "all" else n))]
+        if form is GridGather:
+            outs.append(jax.ShapeDtypeStruct((dp, tensor) + array.shape, array.dtype))
+            mine.append(pltpu.SemaphoreType.DMA)
+        elif form in (LineGather, PairGather):
             outs.append(jax.ShapeDtypeStruct((n,) + array.shape, array.dtype))
             mine.append(pltpu.SemaphoreType.DMA)
+        elif form is GridSum:
+            outs.append(jax.ShapeDtypeStruct(array.shape[2:], jnp.float32))
+            mine.append(pltpu.VMEM(array.shape, array.dtype))
+            mine.append(pltpu.VMEM((2,) + array.shape[1:], array.dtype))
         else:
             outs.append(jax.ShapeDtypeStruct(array.shape[1:], jnp.float32))
-            mine.append(pltpu.VMEM(array.shape, array.dtype))
-            if form is PairSum:
+            if form is LineSum:
+                mine.append(pltpu.VMEM((2,) + array.shape, array.dtype))
+            else:
+                mine.append(pltpu.VMEM(array.shape, array.dtype))
                 mine.append(pltpu.VMEM((n // 2,) + array.shape[1:], array.dtype))
         scratch += mine
         counts.append(len(mine))
     axes = {axis for _, axis, _ in ops}
+    if "all" in axes:
+        axes = {"dp", "tensor"}
 
     def kernel(*refs):
         sources = refs[: len(ops)]
         results = refs[len(ops) : 2 * len(ops)]
         rest = list(refs[2 * len(ops) :])
         d, t = lax.axis_index("dp"), lax.axis_index("tensor")
-        ranks = {"dp": d, "tensor": t, "all": d * tensor + t}
+        ranks = {"dp": d, "tensor": t}
         devices = {
             "dp": lambda i: {"dp": i, "tensor": t},
             "tensor": lambda i: {"dp": d, "tensor": i},
-            "all": lambda i: {"dp": i // tensor, "tensor": lax.rem(i, tensor)},
         }
         barrier = pltpu.get_barrier_semaphore()
-        for axis in ["all"] if "all" in axes else sorted(axes):
+        for axis in sorted(axes):
             n = sizes[axis]
 
             def greet(step, n=n, axis=axis):
@@ -337,17 +507,18 @@
                 )
 
             loop(n - 1, greet)
-        pl.semaphore_wait(
-            barrier,
-            sizes["all"] - 1 if "all" in axes else sum(sizes[axis] - 1 for axis in axes),
-        )
+        pl.semaphore_wait(barrier, sum(sizes[axis] - 1 for axis in axes))
         work = []
         for (form, axis, _), src, out, count in zip(ops, sources, results, counts):
-            work.append(form(sizes[axis], ranks[axis], devices[axis], src, out, *rest[:count]))
+            if axis == "all":
+                work.append(form(dp, tensor, d, t, src, out, *rest[:count]))
+            else:
+                work.append(form(sizes[axis], ranks[axis], devices[axis], src, out, *rest[:count]))
             del rest[:count]
         for op in work:
             op.start()
-        for op in work:
+        order = [GridGather, GridSum, PairSum, LineSum, LineGather, PairGather]
+        for op in sorted(work, key=lambda op: order.index(type(op))):
             op.middle()
         for op in work:
             op.finish()
@@ -413,20 +584,21 @@
         [norm_gain_pair, norm_bias_pair, qv_bias, res_bias, fc_bias.reshape(fc_rows, small)], axis=0
     )
     tiny = pad_to(pad_to(tiny, 1, 128), 0, 16)
-    tokens_all, cot_all, w_attn, w_fc_all, w_proj_all, tiny_all = exchange(
+    tiny_all, tokens_all, cot_all, w_attn, w_fc_all, w_proj_all = exchange(
         dp,
         tensor,
         1,
         [
-            (FlatGather, "tensor", tokens),
-            (FlatGather, "tensor", cotangent),
+            (GridGather, "all", tiny),
+            (LineGather, "tensor", tokens),
+            (LineGather, "tensor", cotangent),
             (PairGather, "dp", pad_to(attention_weights, 0, rows_pad)),
             (PairGather, "dp", pad_to(w_fc, 0, rows_pad)),
             (PairGather, "dp", pad_to(w_proj.T, 0, rows_pad)),
-            (FlatGather, "all", tiny),
         ],
     )
     rows_all = tokens.shape[0] * tensor
+    tiny_all = tiny_all.reshape((devices,) + tiny.shape)
     tokens_all = tokens_all.reshape(rows_all, width)
     cot_all = cot_all.reshape(rows_all, width)
     w_attn = w_attn[:, :rows_own].reshape(width, 4 * local_width)
@@ -463,12 +635,12 @@
     context = context.reshape(rows_all, local_width)
     attn_part = contract_cols(context, w_out_t).astype(half)
     (attn_sum,) = exchange(
-        dp, tensor, 2, [(FlatSum, "tensor", attn_part.reshape(tensor, -1, width))]
+        dp, tensor, 2, [(LineSum, "tensor", attn_part.reshape(tensor, -1, width))]
     )
     first_hidden = residual_stream + attn_sum + res_whole[0]
     second_standardized, second_inverse_deviation = standardize(first_hidden)
     ln2 = (second_standardized * norm_gains[1] + norm_shifts[1]).astype(half)
-    (ln2_all,) = exchange(dp, tensor, 3, [(FlatGather, "tensor", ln2)])
+    (ln2_all,) = exchange(dp, tensor, 3, [(LineGather, "tensor", ln2)])
     ln2_all = ln2_all.reshape(rows_all, width)
     pre = jnp.dot(ln2_all, w_fc_all, preferred_element_type=jnp.float32) + fc_local
     act = gelu_value(pre).astype(half)
@@ -488,8 +660,8 @@
         tensor,
         4,
         [
-            (FlatSum, "tensor", d_ln2_part.reshape(tensor, -1, width)),
-            (FlatSum, "tensor", mlp_part.reshape(tensor, -1, width)),
+            (LineSum, "tensor", d_ln2_part.reshape(tensor, -1, width)),
+            (LineSum, "tensor", mlp_part.reshape(tensor, -1, width)),
             (PairSum, "dp", blocks(proj_grad)),
             (PairSum, "dp", blocks(fc_grad)),
         ],
@@ -504,7 +676,7 @@
     )
     res0_grad = jnp.sum(first_hidden_gradient, axis=0)
     (d_hidden_all,) = exchange(
-        dp, tensor, 5, [(FlatGather, "tensor", first_hidden_gradient.astype(half))]
+        dp, tensor, 5, [(LineGather, "tensor", first_hidden_gradient.astype(half))]
     )
     d_hidden_all = d_hidden_all.reshape(rows_all, width)
     out_grad = contract_rows(d_hidden_all, context)
@@ -544,14 +716,15 @@
         [vector_grads.reshape(8, devices, small).transpose(1, 0, 2), fc_spread], axis=1
     )
     tiny_grads = pad_to(pad_to(tiny_grads, 2, 128), 1, 16)
-    d_ln1, attn_grad_part, tiny_sum = exchange(
+    tiny_grads = tiny_grads.reshape((dp, tensor) + tiny_grads.shape[1:])
+    tiny_sum, d_ln1, attn_grad_part = exchange(
         dp,
         tensor,
         6,
         [
-            (FlatSum, "tensor", d_ln1_part.astype(half).reshape(tensor, -1, width)),
+            (GridSum, "all", tiny_grads),
+            (LineSum, "tensor", d_ln1_part.astype(half).reshape(tensor, -1, width)),
             (PairSum, "dp", blocks(attn_grad)),
-            (FlatSum, "all", tiny_grads),
         ],
     )
     block_input_gradient = (

time: 233 us -> 219 us (0.940)
  Pallas kernels: 178 us -> 161 us
    pallas_call x6, Pallas kernels: 178 us -> 161 us  [exchange(): pl.pallas_call(kernel, out_shape=tuple(outs), in_specs=[pl.BlockSpec(memo...]
    unnamed x124 -> x120, local copies, waits for them, and re-layouts: 13.3 us -> 12.9 us
where the time goes in v2:
time: 219 us; the launch traced here: 218 us
  Pallas kernels  161 us (74%)
  local copies, waits for them, and re-layouts  23.7 us (11%)
  matrix products  20 us (9%)
  other arithmetic  11.4 us (5%)
    pallas_call x6, Pallas kernels, exchange(): pl.pallas_call(kernel, out_shape=tuple(outs), in_specs=[pl.BlockSpec(memo...  161 us
    unnamed x120, local copies, waits for them, and re-layouts  12.9 us

profile of v2, /device:TPU:0, one launch (start us, length us, event | category | flops | bytes accessed | tf_op | source)
XLA Modules:
  0.0 218.2 jit_solution(15616071901418226932)
XLA Ops:
  2.1 0.9 copy.41
  3.0 0.9 slice_bitcast_fusion.6
  4.0 0.9 copy-done
  4.9 0.9 copy-done.2
  5.9 0.9 copy-done.10
  6.8 0.9 copy-done.11
  7.7 38.7 %exchange_1.1 = (f32[8,4,16,128]{3,2,1,0:T(8,128)S(1)}, bf16[4,128,768]{2,1,0:T(8,128)(2,1)S(1)}, bf16[4,128,768]{2,1,0:T(8,128)(2,1)S(1)}, bf16[8,96,768]{2,1,0...) custom-call(f32[16,128]{1,0:T(8,128)S(1)} %pad.39.refs_0_, ...), custom_call_target="tpu_custom_call" | custom-call | tf_op jit(solution)/shard_map/exchange_1/pallas_call | solution.py:526
  46.4 1.0 copy-done.12
  47.4 1.0 copy-done.14
  48.5 0.9 copy-done.16
  54.2 0.9 copy-done.18
  55.1 1.0 convolution_convert_fusion.8
  56.7 25.0 %exchange_2.1 = f32[128,768]{1,0:T(8,128)S(1)} custom-call(bf16[4,128,768]{2,1,0:T(8,128)(2,1)S(1)} %bitcast.104), custom_call_target="tpu_custom_call" | custom-call | tf_op jit(solution)/shard_map/exchange_2/pallas_call | solution.py:526
  83.3 16.1 %exchange_3.1 = bf16[4,128,768]{2,1,0:T(8,128)(2,1)S(1)} custom-call(bf16[128,768]{1,0:T(8,128)(2,1)S(1)} %add_convert_fusion.2.refs_0_), custom_call_target="tpu_custom_call" | custom-call | tf_op jit(solution)/shard_map/exchange_3/pallas_call | solution.py:526
  99.5 2.2 %convolution_add_fusion = f32[512,768]{1,0:T(8,128)S(1)} fusion(bf16[512,768]{1,0:T(8,128)(2,1)S(1)} %bitcast.109, bf16[768,768]{1,0:T(8,128)(2,1)} %bitcast.123, f32[768]{0:T(1024)S(1)} %add.159), kind=kOutput, calls=%fused_computation.23 | convolution fusion | flops 604372992 | bytes 3542016 | tf_op jit(solution)/shard_map/dot_general | solution.py:645
  101.8 2.0 fusion.46
  104.6 1.1 convolution_convert_fusion.3
  105.7 0.9 convolution_convert_fusion.1
  107.5 39.8 %exchange_4.1 = (f32[128,768]{1,0:T(8,128)S(1)}, f32[128,768]{1,0:T(8,128)S(1)}, f32[96,768]{1,0:T(8,128)S(1)}, f32[96,768]{1,0:T(8,128)S(1)}) custom-call(bf16[4,128,768]{2,1,0:T(8,128)(2,1)S(1)} %bitcast.111, bf16[4,128,768]{2,1,0:T(8,128)(2,1)S(1)} %bitcast.112, bf16[8,96,768]{2,1,0:T(8,128)(2,1)S(1)} %bitcast.105, bf16[8,96,768]{2,1,0:T(8,128)(2,1)S(1)} %bitcast.106), custom_call_target="tpu_custom_call" | custom-call | tf_op jit(solution)/shard_map/exchange_4/pallas_call | solution.py:526
  150.5 1.4 add.167
  151.9 2.4 %fusion.38 = (f32[768]{0:T(1024)}, f32[128,768]{1,0:T(8,128)}, bf16[128,768]{1,0:T(8,128)(2,1)}, f32[768]{0:T(1024)}) fusion(f32[128]{0:T(128)} %broadcast_multiply_fusion.4, f32[128,768]{1,0:T(8,128)S(1)} %copy-done.21, f32[128]{0:T(128)} %copy-done.40, f32[128]{0:T(128)} %broadcast_multiply_fusion.5, f32[128,768]{1,0:T(8,128)S(1)} %get-tuple-element.82, ...), kind=kLoop, calls=%fused_computation.113 | loop fusion | flops 1374720 | bytes 1980416 | tf_op jit(solution)/shard_map/reduce_sum | solution.py:677
  155.1 1.0 convert_element_type.108.refs_0_
  156.1 16.1 %exchange_5.1 = bf16[4,128,768]{2,1,0:T(8,128)(2,1)S(1)} custom-call(bf16[128,768]{1,0:T(8,128)(2,1)S(1)} %convert_element_type.108.refs_0_), custom_call_target="tpu_custom_call" | custom-call | tf_op jit(solution)/shard_map/exchange_5/pallas_call | solution.py:526
  172.8 3.1 %fusion.43 = (f32[3,64]{1,0:T(4,128)S(1)}, bf16[512,3,64]{0,2,1:T(8,128)(2,1)S(1)}) fusion(bf16[512,3,64]{0,2,1:T(8,128)(2,1)S(1)} %bitcast.138, f32[3,512,512]{1,2,0:T(8,128)} %copy-done.18, f32[3,512]{1,0:T(4,128)S(1)} %log_add_fusion, pred[512,512]{0,1:T(8,128)(4,1)S(1)} %copy-done.23), kind=kOutput, calls=%fused_computation.117 | convolution fusion | flops 104005440 | bytes 3808000 | tf_op jit(solution)/shard_map/while/body/eval_jaxpr/hqk,qhd->khd/dot_general | solution.py:75
  175.9 1.2 multiply_reduce_fusion
  177.1 1.0 multiply_convert_fusion
  179.6 0.9 fusion.37
  181.8 1.2 copy.50
  183.0 1.6 convolution_convert_fusion.6
  184.6 1.4 copy.49
  187.1 25.8 %exchange_6.1 = (f32[16,128]{1,0:T(8,128)S(1)}, f32[128,768]{1,0:T(8,128)S(1)}, f32[96,768]{1,0:T(8,128)S(1)}) custom-call(f32[8,4,16,128]{3,2,1,0:T(8,128)S(1)} %bitcast.107, bf16[4,128,768]{2,1,0:T(8,128)(2,1)S(1)} %bitcast.108, bf16[8,96,768]{2,1,0:T(8,128)(2,1)S(1)} %pad_maximum_fusion.refs_2_), custom_call_target="tpu_custom_call" | custom-call | tf_op jit(solution)/shard_map/exchange_6/pallas_call | solution.py:526
  213.1 0.9 fusion.25
  (184 shorter events, 22.6 us)
Async XLA Ops:
  49.4 122.9 %copy-start.4 = (bf16[8,96,768]{2,1,0:T(8,128)(2,1)}, bf16[8,96,768]{2,1,0:T(8,128)(2,1)S(1)}, u32[]{:S(2)}) copy-start(bf16[8,96,768]{2,1,0:T(8,128)(2,1)S(1)} %get-tuple-element.77) | copy-start | bytes 3538948
  52.4 1.8 copy-start.32
  52.6 1.5 copy-start.22
  53.4 1.6 copy-start.18
  56.0 25.7 %copy-start.1 = (bf16[128,768]{1,0:T(8,128)(2,1)S(1)}, bf16[128,768]{1,0:T(8,128)(2,1)}, u32[]{:S(2)}) copy-start(bf16[128,768]{1,0:T(8,128)(2,1)} %refs_1_.1) | copy-start | bytes 589828
  82.9 18.8 %copy-start.40 = (f32[128]{0:T(128)}, f32[128]{0:T(128)S(1)}, u32[]{:S(2)}) copy-start(f32[128]{0:T(128)S(1)} %get-tuple-element.175) | copy-start | bytes 1540
  83.1 18.6 %copy-start.49 = (f32[128]{0:T(128)}, f32[128]{0:T(128)S(1)}, u32[]{:S(2)}) copy-start(f32[128]{0:T(128)S(1)} %add_rsqrt_fusion.1) | copy-start | bytes 1540
  99.5 2.2 %copy-start.13 = (bf16[8,96,768]{2,1,0:T(8,128)(2,1)S(1)}, bf16[8,96,768]{2,1,0:T(8,128)(2,1)}, u32[]{:S(2)}) copy-start(bf16[8,96,768]{2,1,0:T(8,128)(2,1)} %copy-done.12) | copy-start | bytes 3538948
  99.5 2.2 %copy-start.17 = (bf16[4,128,768]{2,1,0:T(8,128)(2,1)S(1)}, bf16[4,128,768]{2,1,0:T(8,128)(2,1)}, u32[]{:S(2)}) copy-start(bf16[4,128,768]{2,1,0:T(8,128)(2,1)} %copy-done.16) | copy-start | bytes 2359300
  101.8 2.1 copy-start.15
  107.5 41.2 %copy-start.21 = (f32[128,768]{1,0:T(8,128)S(1)}, f32[128,768]{1,0:T(8,128)}, u32[]{:S(2)}) copy-start(f32[128,768]{1,0:T(8,128)} %copy-done.20) | copy-start | bytes 1179652
  107.5 41.2 %copy-start.41 = (f32[128]{0:T(128)S(1)}, f32[128]{0:T(128)}, u32[]{:S(2)}) copy-start(f32[128]{0:T(128)} %copy-done.40) | copy-start | bytes 1540
  107.5 41.2 %copy-start.50 = (f32[128]{0:T(128)S(1)}, f32[128]{0:T(128)}, u32[]{:S(2)}) copy-start(f32[128]{0:T(128)} %copy-done.49) | copy-start | bytes 1540
  107.5 44.4 %copy-start.3 = (bf16[128,768]{1,0:T(8,128)(2,1)S(1)}, bf16[128,768]{1,0:T(8,128)(2,1)}, u32[]{:S(2)}) copy-start(bf16[128,768]{1,0:T(8,128)(2,1)} %refs_2_.1) | copy-start | bytes 589828
  154.3 18.5 %copy-start.23 = (pred[512,512]{0,1:T(8,128)(4,1)S(1)}, pred[512,512]{0,1:T(8,128)(4,1)}, u32[]{:S(2)}) copy-start(pred[512,512]{0,1:T(8,128)(4,1)} %copy-done.22) | copy-start | bytes 786436
  172.8 3.1 %copy-start.19 = (f32[3,512,512]{1,2,0:T(8,128)S(1)}, f32[3,512,512]{1,2,0:T(8,128)}, u32[]{:S(2)}) copy-start(f32[3,512,512]{1,2,0:T(8,128)} %copy-done.18) | copy-start | bytes 9437188
  172.8 3.1 %copy-start.33 = (bf16[512,192]{0,1:T(8,128)(2,1)S(1)}, bf16[512,192]{0,1:T(8,128)(2,1)}, u32[]{:S(2)}) copy-start(bf16[512,192]{0,1:T(8,128)(2,1)} %copy-done.32) | copy-start | bytes 589828
  175.9 3.6 %copy-start.52 = (bf16[512,3,64]{0,2,1:T(8,128)(2,1)}, bf16[512,3,64]{0,2,1:T(8,128)(2,1)S(1)}, u32[]{:S(2)}) copy-start(bf16[512,3,64]{0,2,1:T(8,128)(2,1)S(1)} %get-tuple-element.140) | copy-start | bytes 589828
  178.1 1.4 copy-start.5
  178.1 1.4 copy-start.44
  178.2 1.4 copy-start.46
  178.8 1.8 copy-start.34
  179.6 1.9 copy-start.37
  179.6 2.0 copy-start.36
  181.4 1.6 copy-start.31
  183.0 3.0 %copy-start.35 = (bf16[3,64,512]{2,1,0:T(8,128)(2,1)S(1)}, bf16[3,64,512]{2,1,0:T(8,128)(2,1)}, u32[]{:S(2)}) copy-start(bf16[3,64,512]{2,1,0:T(8,128)(2,1)} %copy-done.34) | copy-start | bytes 589828
  183.0 3.0 %copy-start.53 = (bf16[512,3,64]{0,2,1:T(8,128)(2,1)S(1)}, bf16[512,3,64]{0,2,1:T(8,128)(2,1)}, u32[]{:S(2)}) copy-start(bf16[512,3,64]{0,2,1:T(8,128)(2,1)} %copy-done.52) | copy-start | bytes 589828
  187.1 25.8 %copy-start.48 = (f32[128]{0:T(128)S(1)}, f32[128]{0:T(128)}, u32[]{:S(2)}) copy-start(f32[128]{0:T(128)} %copy-done.47) | copy-start | bytes 1540
  187.1 25.8 %copy-start.51 = (f32[128]{0:T(128)S(1)}, f32[128]{0:T(128)}, u32[]{:S(2)}) copy-start(f32[128]{0:T(128)} %get-tuple-element.174) | copy-start | bytes 1540
  187.1 26.0 %copy-start.24 = (f32[128,768]{1,0:T(8,128)S(1)}, f32[128,768]{1,0:T(8,128)}, u32[]{:S(2)}) copy-start(f32[128,768]{1,0:T(8,128)} %get-tuple-element.130) | copy-start | bytes 1179652
  212.9 3.9 %copy-start.9 = (f32[96,768]{1,0:T(8,128)S(1)}, f32[96,768]{1,0:T(8,128)}, u32[]{:S(2)}) copy-start(f32[96,768]{1,0:T(8,128)} %copy-done.8) | copy-start | bytes 884740
  213.1 4.4 %copy-start.7 = (f32[96,768]{1,0:T(8,128)S(1)}, f32[96,768]{1,0:T(8,128)}, u32[]{:S(2)}) copy-start(f32[96,768]{1,0:T(8,128)} %copy-done.6) | copy-start | bytes 884740
  (22 other events, 19.9 us)

commit v3 on v2

--- a/solution.py
+++ b/solution.py
@@ -272,72 +272,36 @@
         self.local.wait()
 
 
-class LineSum:
+class FlatSum:
     def __init__(self, n, me, device, src, out, sems, slots):
         self.n, self.me, self.device, self.src, self.out, self.sems = n, me, device, src, out, sems
         self.slots = slots
 
-    def move(self, side, block, first=False):
-        peer = lax.rem(self.me + (1 if side == 0 else self.n - 1), self.n)
-        return remote(
-            self.src.at[block] if first else self.slots.at[side, block],
-            self.slots.at[side, block],
-            self.sems.at[2 * side, block],
-            self.sems.at[2 * side + 1, block],
+    def copy(self, step):
+        k = step + 1
+        peer = lax.rem(self.me + k, self.n)
+        return remote(
+            self.src.at[peer],
+            self.slots.at[k],
+            self.sems.at[0, k],
+            self.sems.at[1, k],
             self.device(peer),
         )
 
     def start(self):
-        @pl.when(self.me == 0)
-        def _():
-            for step in range(self.n - 1):
-                self.move(0, self.n - 1 - step, True).start()
-
-        @pl.when(self.me == self.n - 1)
-        def _():
-            for step in range(self.n - 1):
-                self.move(1, step, True).start()
-
-    def forward(self, side, block):
-        self.move(side, block).wait_recv()
-        self.slots[side, block] = (
-            self.slots[side, block].astype(jnp.float32) + self.src[block].astype(jnp.float32)
-        ).astype(self.slots.dtype)
-        self.move(side, block).start()
+        loop(self.n - 1, lambda step: self.copy(step).start())
 
     def middle(self):
-        for step in range(self.n - 1):
-
-            @pl.when((self.me > 0) & (self.me < self.n - 1 - step))
-            def _():
-                self.forward(0, self.n - 1 - step)
-
-            @pl.when((self.me < self.n - 1) & (self.me > step))
-            def _():
-                self.forward(1, step)
+        pass
 
     def finish(self):
         self.out[...] = self.src[self.me].astype(jnp.float32)
 
-        @pl.when(self.me > 0)
-        def _():
-            self.move(0, self.me).wait_recv()
-            self.out[...] += self.slots[0, self.me].astype(jnp.float32)
-
-        @pl.when(self.me < self.n - 1)
-        def _():
-            self.move(1, self.me).wait_recv()
-            self.out[...] += self.slots[1, self.me].astype(jnp.float32)
-
-        for block in range(self.n):
-
-            @pl.when(self.me < block)
-            def _():
-                self.move(0, block).wait_send()
-
-            @pl.when(self.me > block)
-            def _():
-                self.move(1, block).wait_send()
+        def add(step):
+            self.copy(step).wait()
+            self.out[...] += self.slots[step + 1].astype(jnp.float32)
+
+        loop(self.n - 1, add)
 
 
 class PairGather:
@@ -473,10 +437,8 @@
             mine.append(pltpu.VMEM((2,) + array.shape[1:], array.dtype))
         else:
             outs.append(jax.ShapeDtypeStruct(array.shape[1:], jnp.float32))
-            if form is LineSum:
-                mine.append(pltpu.VMEM((2,) + array.shape, array.dtype))
-            else:
-                mine.append(pltpu.VMEM(array.shape, array.dtype))
+            mine.append(pltpu.VMEM(array.shape, array.dtype))
+            if form is PairSum:
                 mine.append(pltpu.VMEM((n // 2,) + array.shape[1:], array.dtype))
         scratch += mine
         counts.append(len(mine))
@@ -517,7 +479,7 @@
             del rest[:count]
         for op in work:
             op.start()
-        order = [GridGather, GridSum, PairSum, LineSum, LineGather, PairGather]
+        order = [GridGather, GridSum, PairSum, FlatSum, LineGather, PairGather]
         for op in sorted(work, key=lambda op: order.index(type(op))):
             op.middle()
         for op in work:
@@ -584,26 +546,20 @@
         [norm_gain_pair, norm_bias_pair, qv_bias, res_bias, fc_bias.reshape(fc_rows, small)], axis=0
     )
     tiny = pad_to(pad_to(tiny, 1, 128), 0, 16)
-    tiny_all, tokens_all, cot_all, w_attn, w_fc_all, w_proj_all = exchange(
+    tiny_all, tokens_all, w_attn = exchange(
         dp,
         tensor,
         1,
         [
             (GridGather, "all", tiny),
             (LineGather, "tensor", tokens),
-            (LineGather, "tensor", cotangent),
             (PairGather, "dp", pad_to(attention_weights, 0, rows_pad)),
-            (PairGather, "dp", pad_to(w_fc, 0, rows_pad)),
-            (PairGather, "dp", pad_to(w_proj.T, 0, rows_pad)),
         ],
     )
     rows_all = tokens.shape[0] * tensor
     tiny_all = tiny_all.reshape((devices,) + tiny.shape)
     tokens_all = tokens_all.reshape(rows_all, width)
-    cot_all = cot_all.reshape(rows_all, width)
     w_attn = w_attn[:, :rows_own].reshape(width, 4 * local_width)
-    w_fc_all = w_fc_all[:, :rows_own].reshape(width, local_hidden)
-    w_proj_all = w_proj_all[:, :rows_own].reshape(width, local_hidden)
     w_in, w_out_t = w_attn[:, : 3 * local_width], w_attn[:, 3 * local_width :]
     vectors = tiny_all[:, :8, :small].transpose(1, 0, 2).reshape(8, width)
     norm_gains, norm_shifts, qv_whole, res_whole = (
@@ -634,9 +590,20 @@
     context, logsum = lax.map(attend, (query, keys, value, segments))
     context = context.reshape(rows_all, local_width)
     attn_part = contract_cols(context, w_out_t).astype(half)
-    (attn_sum,) = exchange(
-        dp, tensor, 2, [(LineSum, "tensor", attn_part.reshape(tensor, -1, width))]
-    )
+    attn_sum, cot_all, w_fc_all, w_proj_all = exchange(
+        dp,
+        tensor,
+        2,
+        [
+            (FlatSum, "tensor", attn_part.reshape(tensor, -1, width)),
+            (LineGather, "tensor", cotangent),
+            (PairGather, "dp", pad_to(w_fc, 0, rows_pad)),
+            (PairGather, "dp", pad_to(w_proj.T, 0, rows_pad)),
+        ],
+    )
+    cot_all = cot_all.reshape(rows_all, width)
+    w_fc_all = w_fc_all[:, :rows_own].reshape(width, local_hidden)
+    w_proj_all = w_proj_all[:, :rows_own].reshape(width, local_hidden)
     first_hidden = residual_stream + attn_sum + res_whole[0]
     second_standardized, second_inverse_deviation = standardize(first_hidden)
     ln2 = (second_standardized * norm_gains[1] + norm_shifts[1]).astype(half)
@@ -655,18 +622,15 @@
     def blocks(array):
         return pad_to(array.reshape(dp, rows_own, array.shape[1]), 1, rows_pad)
 
-    d_ln2, mlp_sum, proj_part, fc_part = exchange(
+    d_ln2, proj_part = exchange(
         dp,
         tensor,
         4,
         [
-            (LineSum, "tensor", d_ln2_part.reshape(tensor, -1, width)),
-            (LineSum, "tensor", mlp_part.reshape(tensor, -1, width)),
+            (FlatSum, "tensor", d_ln2_part.reshape(tensor, -1, width)),
             (PairSum, "dp", blocks(proj_grad)),
-            (PairSum, "dp", blocks(fc_grad)),
         ],
     )
-    block_out = (first_hidden + mlp_sum + res_whole[1]).astype(half)
     residual_gradient = cotangent.astype(jnp.float32)
     res1_grad = jnp.sum(residual_gradient, axis=0)
     second_gain_gradient = jnp.sum(d_ln2 * second_standardized, axis=0)
@@ -675,9 +639,17 @@
         d_ln2, second_standardized, second_inverse_deviation, norm_gains[1]
     )
     res0_grad = jnp.sum(first_hidden_gradient, axis=0)
-    (d_hidden_all,) = exchange(
-        dp, tensor, 5, [(LineGather, "tensor", first_hidden_gradient.astype(half))]
-    )
+    d_hidden_all, mlp_sum, fc_part = exchange(
+        dp,
+        tensor,
+        5,
+        [
+            (LineGather, "tensor", first_hidden_gradient.astype(half)),
+            (FlatSum, "tensor", mlp_part.reshape(tensor, -1, width)),
+            (PairSum, "dp", blocks(fc_grad)),
+        ],
+    )
+    block_out = (first_hidden + mlp_sum + res_whole[1]).astype(half)
     d_hidden_all = d_hidden_all.reshape(rows_all, width)
     out_grad = contract_rows(d_hidden_all, context)
     d_context = jnp.dot(d_hidden_all, w_out_t, preferred_element_type=jnp.float32).astype(half)
@@ -723,7 +695,7 @@
         6,
         [
             (GridSum, "all", tiny_grads),
-            (LineSum, "tensor", d_ln1_part.astype(half).reshape(tensor, -1, width)),
+            (FlatSum, "tensor", d_ln1_part.astype(half).reshape(tensor, -1, width)),
             (PairSum, "dp", blocks(attn_grad)),
         ],
     )

time: 219 us -> 204 us (0.932)
  local copies, waits for them, and re-layouts: 23.7 us -> 18.1 us
  Pallas kernels: 161 us -> 157 us
  other arithmetic: 11.4 us -> 7.91 us
    pallas_call x6, Pallas kernels: 161 us -> 157 us  [exchange(): pl.pallas_call(kernel, out_shape=tuple(outs), in_specs=[pl.BlockSpec(memo...]
    unnamed x120 -> x90, local copies, waits for them, and re-layouts: 12.9 us -> 10.1 us
where the time goes in v3:
time: 204 us
  Pallas kernels  157 us (77%)
  matrix products  19.4 us (10%)
  local copies, waits for them, and re-layouts  18.1 us (9%)
  other arithmetic  7.91 us (4%)
    pallas_call x6, Pallas kernels, exchange(): pl.pallas_call(kernel, out_shape=tuple(outs), in_specs=[pl.BlockSpec(memo...  157 us
    unnamed x90, local copies, waits for them, and re-layouts  10.1 us
    dot_general x4, matrix products, contract_rows(): lax.dot_general(left, right, (((0,), (0,)), ((), ())), preferred_element_...  4.11 us

profile of v3, /device:TPU:0, one launch (start us, length us, event | category | flops | bytes accessed | tf_op | source)
XLA Modules:
  0.0 203.7 jit_solution(118759481256699268)
XLA Ops:
  1.4 0.8 concatenate.22
  2.1 0.9 copy.41
  3.0 0.9 slice_bitcast_fusion.6
  4.0 0.9 copy-done
  4.9 25.3 %exchange_1.1 = (f32[8,4,16,128]{3,2,1,0:T(8,128)S(1)}, bf16[4,128,768]{2,1,0:T(8,128)(2,1)S(1)}, bf16[8,96,768]{2,1,0:T(8,128)(2,1)S(1)}) custom-call(f32[16,128]{1,0:T(8,128)S(1)} %pad.39.refs_0_, bf16[128,768]{1,0:T(8,128)(2,1)S(1)} %copy-done, bf16[96,768]{1,0:T(8,128)(2,1)S(1)} %pad_maximum_fusion.6.refs_2_), custom_call_target="tpu_custom_call" | custom-call | tf_op jit(solution)/shard_map/exchange_1/pallas_call | solution.py:488
  32.9 0.8 fusion
  34.4 0.9 copy-done.17
  35.3 1.0 convolution_convert_fusion.8
  37.0 37.5 %exchange_2.1 = (f32[128,768]{1,0:T(8,128)S(1)}, bf16[4,128,768]{2,1,0:T(8,128)(2,1)S(1)}, bf16[8,96,768]{2,1,0:T(8,128)(2,1)S(1)}, bf16[8,96,768]{2,1,0:T(8,128)(2,1)S(1)}) custom-call(bf16[4,128,768]{2,1,0:T(8,128)(2,1)S(1)} %bitcast.104, bf16[128,768]{1,0:T(8,128)(2,1)S(1)} %copy-done.2, bf16[96,768]{1,0:T(8,128)(2,1)S(1)} %copy-done.9, ...), custom_call_target="tpu_custom_call" | custom-call | tf_op jit(solution)/shard_map/exchange_2/pallas_call | solution.py:488
  74.5 1.0 copy-done.13
  75.5 0.9 copy-done.15
  78.4 18.9 %exchange_3.1 = bf16[4,128,768]{2,1,0:T(8,128)(2,1)S(1)} custom-call(bf16[128,768]{1,0:T(8,128)(2,1)S(1)} %add_convert_fusion.2.refs_0_), custom_call_target="tpu_custom_call" | custom-call | tf_op jit(solution)/shard_map/exchange_3/pallas_call | solution.py:488
  97.5 2.2 %convolution_add_fusion = f32[512,768]{1,0:T(8,128)S(1)} fusion(bf16[512,768]{1,0:T(8,128)(2,1)S(1)} %bitcast.110, bf16[768,768]{1,0:T(8,128)(2,1)} %bitcast.123, f32[768]{0:T(1024)S(1)} %add.159), kind=kOutput, calls=%fused_computation.23 | convolution fusion | flops 604372992 | bytes 3542016 | tf_op jit(solution)/shard_map/dot_general | solution.py:612
  99.7 1.4 fusion.46
  101.1 0.8 convolution_convert_fusion.4
  101.9 0.9 convolution_convert_fusion.1
  102.9 16.4 %exchange_4.1 = (f32[128,768]{1,0:T(8,128)S(1)}, f32[96,768]{1,0:T(8,128)S(1)}) custom-call(bf16[4,128,768]{2,1,0:T(8,128)(2,1)S(1)} %bitcast.112, bf16[8,96,768]{2,1,0:T(8,128)(2,1)S(1)} %bitcast.106), custom_call_target="tpu_custom_call" | custom-call | tf_op jit(solution)/shard_map/exchange_4/pallas_call | solution.py:488
  120.6 1.1 convolution_convert_fusion.3
  121.7 0.8 convolution_convert_fusion
  122.5 35.4 %exchange_5.1 = (bf16[4,128,768]{2,1,0:T(8,128)(2,1)S(1)}, f32[128,768]{1,0:T(8,128)S(1)}, f32[96,768]{1,0:T(8,128)S(1)}) custom-call(bf16[128,768]{1,0:T(8,128)(2,1)S(1)} %convert_element_type.105.refs_0_, bf16[4,128,768]{2,1,0:T(8,128)(2,1)S(1)} %bitcast.109, bf16[8,96,768]{2,1,0:T(8,128)(2,1)S(1)} %bitcast.105), custom_call_target="tpu_custom_call" | custom-call | tf_op jit(solution)/shard_map/exchange_5/pallas_call | solution.py:488
  158.7 1.7 add_convert_fusion.1
  161.2 3.1 %fusion.43 = (f32[3,64]{1,0:T(4,128)S(1)}, bf16[512,3,64]{0,2,1:T(8,128)(2,1)S(1)}) fusion(bf16[512,3,64]{0,2,1:T(8,128)(2,1)S(1)} %bitcast.138, f32[3,512,512]{1,2,0:T(8,128)} %copy-done.17, f32[3,512]{1,0:T(4,128)S(1)} %log_add_fusion, pred[512,512]{0,1:T(8,128)(4,1)} %copy-done.21), kind=kOutput, calls=%fused_computation.117 | convolution fusion | flops 104005440 | bytes 3808000 | tf_op jit(solution)/shard_map/while/body/eval_jaxpr/hqk,qhd->khd/dot_general | solution.py:75
  164.3 1.2 multiply_reduce_fusion
  165.5 1.0 multiply_convert_fusion
  167.9 0.9 fusion.37
  170.1 1.2 copy.50
  171.2 1.6 convolution_convert_fusion.6
  172.8 1.4 copy.49
  174.2 0.8 convolution_convert_fusion.2
  175.3 23.0 %exchange_6.1 = (f32[16,128]{1,0:T(8,128)S(1)}, f32[128,768]{1,0:T(8,128)S(1)}, f32[96,768]{1,0:T(8,128)S(1)}) custom-call(f32[8,4,16,128]{3,2,1,0:T(8,128)S(1)} %bitcast.107, bf16[4,128,768]{2,1,0:T(8,128)(2,1)S(1)} %bitcast.108, bf16[8,96,768]{2,1,0:T(8,128)(2,1)S(1)} %pad_maximum_fusion.refs_2_), custom_call_target="tpu_custom_call" | custom-call | tf_op jit(solution)/shard_map/exchange_6/pallas_call | solution.py:488
  198.6 0.9 fusion.25
  200.1 0.7 pad_maximum_fusion.2
  (155 shorter events, 15.8 us)
Async XLA Ops:
  4.0 0.9 copy-start
  30.3 130.2 %copy-start.3 = (bf16[8,96,768]{2,1,0:T(8,128)(2,1)}, bf16[8,96,768]{2,1,0:T(8,128)(2,1)S(1)}, u32[]{:S(2)}) copy-start(bf16[8,96,768]{2,1,0:T(8,128)(2,1)S(1)} %get-tuple-element.79) | copy-start | bytes 3538948
  31.6 1.0 copy-start.25
  32.6 1.0 copy-start.26
  32.6 1.0 copy-start.28
  32.6 1.8 copy-start.32
  32.8 1.5 copy-start.21
  33.6 1.7 copy-start.17
  35.3 1.7 copy-start.2
  35.3 1.7 copy-start.9
  35.3 1.7 copy-start.10
  36.3 40.1 %copy-start.1 = (bf16[128,768]{1,0:T(8,128)(2,1)S(1)}, bf16[128,768]{1,0:T(8,128)(2,1)}, u32[]{:S(2)}) copy-start(bf16[128,768]{1,0:T(8,128)(2,1)} %refs_1_.2) | copy-start | bytes 589828
  74.5 1.0 copy-start.13
  76.4 1.0 copy-start.11
  97.4 2.2 %copy-start.12 = (bf16[8,96,768]{2,1,0:T(8,128)(2,1)S(1)}, bf16[8,96,768]{2,1,0:T(8,128)(2,1)}, u32[]{:S(2)}) copy-start(bf16[8,96,768]{2,1,0:T(8,128)(2,1)} %copy-done.11) | copy-start | bytes 3538948
  97.4 2.2 %copy-start.16 = (bf16[4,128,768]{2,1,0:T(8,128)(2,1)S(1)}, bf16[4,128,768]{2,1,0:T(8,128)(2,1)}, u32[]{:S(2)}) copy-start(bf16[4,128,768]{2,1,0:T(8,128)(2,1)} %copy-done.15) | copy-start | bytes 2359300
  99.7 1.5 copy-start.14
  102.9 16.4 %copy-start.20 = (f32[128,768]{1,0:T(8,128)S(1)}, f32[128,768]{1,0:T(8,128)}, u32[]{:S(2)}) copy-start(f32[128,768]{1,0:T(8,128)} %copy-done.19) | copy-start | bytes 1179652
  119.3 2.3 %copy-start.5 = (f32[96,768]{1,0:T(8,128)}, f32[96,768]{1,0:T(8,128)S(1)}, u32[]{:S(2)}) copy-start(f32[96,768]{1,0:T(8,128)S(1)} %get-tuple-element.91) | copy-start | bytes 884740
  161.1 3.1 %copy-start.18 = (f32[3,512,512]{1,2,0:T(8,128)S(1)}, f32[3,512,512]{1,2,0:T(8,128)}, u32[]{:S(2)}) copy-start(f32[3,512,512]{1,2,0:T(8,128)} %copy-done.17) | copy-start | bytes 9437188
  161.1 3.1 %copy-start.22 = (pred[512,512]{0,1:T(8,128)(4,1)S(1)}, pred[512,512]{0,1:T(8,128)(4,1)}, u32[]{:S(2)}) copy-start(pred[512,512]{0,1:T(8,128)(4,1)} %copy-done.21) | copy-start | bytes 786436
  161.1 3.1 %copy-start.33 = (bf16[512,192]{0,1:T(8,128)(2,1)S(1)}, bf16[512,192]{0,1:T(8,128)(2,1)}, u32[]{:S(2)}) copy-start(bf16[512,192]{0,1:T(8,128)(2,1)} %copy-done.32) | copy-start | bytes 589828
  164.2 3.6 %copy-start.37 = (bf16[512,3,64]{0,2,1:T(8,128)(2,1)}, bf16[512,3,64]{0,2,1:T(8,128)(2,1)S(1)}, u32[]{:S(2)}) copy-start(bf16[512,3,64]{0,2,1:T(8,128)(2,1)S(1)} %get-tuple-element.144) | copy-start | bytes 589828
  165.4 1.0 copy-start.29
  166.5 1.4 copy-start.4
  167.1 1.7 copy-start.34
  169.7 1.6 copy-start.31
  171.2 3.0 %copy-start.35 = (bf16[3,64,512]{2,1,0:T(8,128)(2,1)S(1)}, bf16[3,64,512]{2,1,0:T(8,128)(2,1)}, u32[]{:S(2)}) copy-start(bf16[3,64,512]{2,1,0:T(8,128)(2,1)} %copy-done.34) | copy-start | bytes 589828
  171.2 3.0 %copy-start.38 = (bf16[512,3,64]{0,2,1:T(8,128)(2,1)S(1)}, bf16[512,3,64]{0,2,1:T(8,128)(2,1)}, u32[]{:S(2)}) copy-start(bf16[512,3,64]{0,2,1:T(8,128)(2,1)} %copy-done.37) | copy-start | bytes 589828
  175.3 23.3 %copy-start.24 = (f32[128,768]{1,0:T(8,128)S(1)}, f32[128,768]{1,0:T(8,128)}, u32[]{:S(2)}) copy-start(f32[128,768]{1,0:T(8,128)} %copy-done.23) | copy-start | bytes 1179652
  198.3 3.9 %copy-start.8 = (f32[96,768]{1,0:T(8,128)S(1)}, f32[96,768]{1,0:T(8,128)}, u32[]{:S(2)}) copy-start(f32[96,768]{1,0:T(8,128)} %copy-done.7) | copy-start | bytes 884740
  198.6 4.4 %copy-start.6 = (f32[96,768]{1,0:T(8,128)S(1)}, f32[96,768]{1,0:T(8,128)}, u32[]{:S(2)}) copy-start(f32[96,768]{1,0:T(8,128)} %copy-done.5) | copy-start | bytes 884740
  (7 other events, 5.5 us)

commit v4 on v3

--- a/solution.py
+++ b/solution.py
@@ -590,24 +590,25 @@
     context, logsum = lax.map(attend, (query, keys, value, segments))
     context = context.reshape(rows_all, local_width)
     attn_part = contract_cols(context, w_out_t).astype(half)
-    attn_sum, cot_all, w_fc_all, w_proj_all = exchange(
+    attn_sum, w_fc_all, w_proj_all = exchange(
         dp,
         tensor,
         2,
         [
             (FlatSum, "tensor", attn_part.reshape(tensor, -1, width)),
-            (LineGather, "tensor", cotangent),
             (PairGather, "dp", pad_to(w_fc, 0, rows_pad)),
             (PairGather, "dp", pad_to(w_proj.T, 0, rows_pad)),
         ],
     )
-    cot_all = cot_all.reshape(rows_all, width)
     w_fc_all = w_fc_all[:, :rows_own].reshape(width, local_hidden)
     w_proj_all = w_proj_all[:, :rows_own].reshape(width, local_hidden)
     first_hidden = residual_stream + attn_sum + res_whole[0]
     second_standardized, second_inverse_deviation = standardize(first_hidden)
     ln2 = (second_standardized * norm_gains[1] + norm_shifts[1]).astype(half)
-    (ln2_all,) = exchange(dp, tensor, 3, [(LineGather, "tensor", ln2)])
+    ln2_all, cot_all = exchange(
+        dp, tensor, 3, [(LineGather, "tensor", ln2), (LineGather, "tensor", cotangent)]
+    )
+    cot_all = cot_all.reshape(rows_all, width)
     ln2_all = ln2_all.reshape(rows_all, width)
     pre = jnp.dot(ln2_all, w_fc_all, preferred_element_type=jnp.float32) + fc_local
     act = gelu_value(pre).astype(half)

time: 204 us -> 198 us (0.971)
  Pallas kernels: 157 us -> 151 us
    pallas_call x6, Pallas kernels: 157 us -> 151 us  [exchange(): pl.pallas_call(kernel, out_shape=tuple(outs), in_specs=[pl.BlockSpec(memo...]
where the time goes in v4:
time: 198 us
  Pallas kernels  151 us (76%)
  matrix products  19.4 us (10%)
  local copies, waits for them, and re-layouts  18.1 us (9%)
  other arithmetic  7.91 us (4%)
    pallas_call x6, Pallas kernels, exchange(): pl.pallas_call(kernel, out_shape=tuple(outs), in_specs=[pl.BlockSpec(memo...  151 us
    unnamed x90, local copies, waits for them, and re-layouts  10.1 us
    dot_general x4, matrix products, contract_rows(): lax.dot_general(left, right, (((0,), (0,)), ((), ())), preferred_element_...  4.11 us

profile of v4, /device:TPU:0, one launch (start us, length us, event | category | flops | bytes accessed | tf_op | source)
XLA Modules:
  0.0 198.0 jit_solution(1367226911815208373)
XLA Ops:
  1.4 0.8 concatenate.22
  2.1 0.9 copy.41
  3.0 0.9 slice_bitcast_fusion.6
  4.0 0.9 copy-done
  4.9 25.3 %exchange_1.1 = (f32[8,4,16,128]{3,2,1,0:T(8,128)S(1)}, bf16[4,128,768]{2,1,0:T(8,128)(2,1)S(1)}, bf16[8,96,768]{2,1,0:T(8,128)(2,1)S(1)}) custom-call(f32[16,128]{1,0:T(8,128)S(1)} %pad.39.refs_0_, bf16[128,768]{1,0:T(8,128)(2,1)S(1)} %copy-done, bf16[96,768]{1,0:T(8,128)(2,1)S(1)} %pad_maximum_fusion.6.refs_2_), custom_call_target="tpu_custom_call" | custom-call | tf_op jit(solution)/shard_map/exchange_1/pallas_call | solution.py:488
  32.9 0.8 fusion
  34.4 0.9 copy-done.17
  35.3 1.0 convolution_convert_fusion.8
  37.0 18.0 %exchange_2.1 = (f32[128,768]{1,0:T(8,128)S(1)}, bf16[8,96,768]{2,1,0:T(8,128)(2,1)S(1)}, bf16[8,96,768]{2,1,0:T(8,128)(2,1)S(1)}) custom-call(bf16[4,128,768]{2,1,0:T(8,128)(2,1)S(1)} %bitcast.104, bf16[96,768]{1,0:T(8,128)(2,1)S(1)} %copy-done.9, bf16[96,768]{1,0:T(8,128)(2,1)S(1)} %bitcast.116), custom_call_target="tpu_custom_call" | custom-call | tf_op jit(solution)/shard_map/exchange_2/pallas_call | solution.py:488
  55.0 1.0 copy-done.13
  58.0 31.5 %exchange_3.1 = (bf16[4,128,768]{2,1,0:T(8,128)(2,1)S(1)}, bf16[4,128,768]{2,1,0:T(8,128)(2,1)S(1)}) custom-call(bf16[128,768]{1,0:T(8,128)(2,1)S(1)} %add_convert_fusion.2.refs_0_, bf16[128,768]{1,0:T(8,128)(2,1)S(1)} %copy-done.2), custom_call_target="tpu_custom_call" | custom-call | tf_op jit(solution)/shard_map/exchange_3/pallas_call | solution.py:488
  89.5 0.9 copy-done.15
  90.5 2.2 %convolution_add_fusion = f32[512,768]{1,0:T(8,128)S(1)} fusion(bf16[512,768]{1,0:T(8,128)(2,1)S(1)} %bitcast.123, bf16[768,768]{1,0:T(8,128)(2,1)} %bitcast.121, f32[768]{0:T(1024)S(1)} %add.159), kind=kOutput, calls=%fused_computation.23 | convolution fusion | flops 604372992 | bytes 3542016 | tf_op jit(solution)/shard_map/dot_general | solution.py:613
  92.7 1.4 fusion.46
  94.2 0.8 convolution_convert_fusion.4
  95.0 0.9 convolution_convert_fusion.1
  96.0 17.4 %exchange_4.1 = (f32[128,768]{1,0:T(8,128)S(1)}, f32[96,768]{1,0:T(8,128)S(1)}) custom-call(bf16[4,128,768]{2,1,0:T(8,128)(2,1)S(1)} %bitcast.110, bf16[8,96,768]{2,1,0:T(8,128)(2,1)S(1)} %bitcast.106), custom_call_target="tpu_custom_call" | custom-call | tf_op jit(solution)/shard_map/exchange_4/pallas_call | solution.py:488
  114.6 1.1 convolution_convert_fusion.3
  115.7 0.8 convolution_convert_fusion
  116.5 35.8 %exchange_5.1 = (bf16[4,128,768]{2,1,0:T(8,128)(2,1)S(1)}, f32[128,768]{1,0:T(8,128)S(1)}, f32[96,768]{1,0:T(8,128)S(1)}) custom-call(bf16[128,768]{1,0:T(8,128)(2,1)S(1)} %convert_element_type.105.refs_0_, bf16[4,128,768]{2,1,0:T(8,128)(2,1)S(1)} %bitcast.109, bf16[8,96,768]{2,1,0:T(8,128)(2,1)S(1)} %bitcast.105), custom_call_target="tpu_custom_call" | custom-call | tf_op jit(solution)/shard_map/exchange_5/pallas_call | solution.py:488
  153.1 1.7 add_convert_fusion.1
  155.6 3.1 %fusion.43 = (f32[3,64]{1,0:T(4,128)S(1)}, bf16[512,3,64]{0,2,1:T(8,128)(2,1)S(1)}) fusion(bf16[512,3,64]{0,2,1:T(8,128)(2,1)S(1)} %bitcast.138, f32[3,512,512]{1,2,0:T(8,128)} %copy-done.17, f32[3,512]{1,0:T(4,128)S(1)} %log_add_fusion, pred[512,512]{0,1:T(8,128)(4,1)} %copy-done.21), kind=kOutput, calls=%fused_computation.117 | convolution fusion | flops 104005440 | bytes 3808000 | tf_op jit(solution)/shard_map/while/body/eval_jaxpr/hqk,qhd->khd/dot_general | solution.py:75
  158.7 1.2 multiply_reduce_fusion
  159.9 1.0 multiply_convert_fusion
  162.3 0.9 fusion.37
  164.5 1.2 copy.50
  165.6 1.6 convolution_convert_fusion.6
  167.2 1.4 copy.49
  168.6 0.8 convolution_convert_fusion.2
  169.7 22.9 %exchange_6.1 = (f32[16,128]{1,0:T(8,128)S(1)}, f32[128,768]{1,0:T(8,128)S(1)}, f32[96,768]{1,0:T(8,128)S(1)}) custom-call(f32[8,4,16,128]{3,2,1,0:T(8,128)S(1)} %bitcast.107, bf16[4,128,768]{2,1,0:T(8,128)(2,1)S(1)} %bitcast.108, bf16[8,96,768]{2,1,0:T(8,128)(2,1)S(1)} %pad_maximum_fusion.refs_2_), custom_call_target="tpu_custom_call" | custom-call | tf_op jit(solution)/shard_map/exchange_6/pallas_call | solution.py:488
  192.9 0.9 fusion.25
  194.5 0.7 pad_maximum_fusion.2
  (155 shorter events, 15.8 us)
Async XLA Ops:
  4.0 0.9 copy-start
  30.3 124.7 %copy-start.3 = (bf16[8,96,768]{2,1,0:T(8,128)(2,1)}, bf16[8,96,768]{2,1,0:T(8,128)(2,1)S(1)}, u32[]{:S(2)}) copy-start(bf16[8,96,768]{2,1,0:T(8,128)(2,1)S(1)} %get-tuple-element.80) | copy-start | bytes 3538948
  31.6 1.0 copy-start.25
  32.6 1.0 copy-start.26
  32.6 1.0 copy-start.28
  32.6 1.8 copy-start.32
  32.8 1.5 copy-start.21
  33.6 1.7 copy-start.17
  35.3 1.7 copy-start.9
  35.3 1.7 copy-start.10
  36.3 19.8 %copy-start.1 = (bf16[128,768]{1,0:T(8,128)(2,1)S(1)}, bf16[128,768]{1,0:T(8,128)(2,1)}, u32[]{:S(2)}) copy-start(bf16[128,768]{1,0:T(8,128)(2,1)} %refs_1_.3) | copy-start | bytes 589828
  37.0 21.1 %copy-start.2 = (bf16[128,768]{1,0:T(8,128)(2,1)S(1)}, bf16[128,768]{1,0:T(8,128)(2,1)}, u32[]{:S(2)}) copy-start(bf16[128,768]{1,0:T(8,128)(2,1)} %refs_1_.5) | copy-start | bytes 589828
  55.0 1.0 copy-start.13
  56.1 1.0 copy-start.11
  90.5 2.2 %copy-start.12 = (bf16[8,96,768]{2,1,0:T(8,128)(2,1)S(1)}, bf16[8,96,768]{2,1,0:T(8,128)(2,1)}, u32[]{:S(2)}) copy-start(bf16[8,96,768]{2,1,0:T(8,128)(2,1)} %copy-done.11) | copy-start | bytes 3538948
  90.5 2.2 %copy-start.16 = (bf16[4,128,768]{2,1,0:T(8,128)(2,1)S(1)}, bf16[4,128,768]{2,1,0:T(8,128)(2,1)}, u32[]{:S(2)}) copy-start(bf16[4,128,768]{2,1,0:T(8,128)(2,1)} %copy-done.15) | copy-start | bytes 2359300
  92.7 1.5 copy-start.14
  95.9 17.4 %copy-start.20 = (f32[128,768]{1,0:T(8,128)S(1)}, f32[128,768]{1,0:T(8,128)}, u32[]{:S(2)}) copy-start(f32[128,768]{1,0:T(8,128)} %copy-done.19) | copy-start | bytes 1179652
  113.4 2.3 %copy-start.5 = (f32[96,768]{1,0:T(8,128)}, f32[96,768]{1,0:T(8,128)S(1)}, u32[]{:S(2)}) copy-start(f32[96,768]{1,0:T(8,128)S(1)} %get-tuple-element.93) | copy-start | bytes 884740
  155.5 3.1 %copy-start.18 = (f32[3,512,512]{1,2,0:T(8,128)S(1)}, f32[3,512,512]{1,2,0:T(8,128)}, u32[]{:S(2)}) copy-start(f32[3,512,512]{1,2,0:T(8,128)} %copy-done.17) | copy-start | bytes 9437188
  155.5 3.1 %copy-start.22 = (pred[512,512]{0,1:T(8,128)(4,1)S(1)}, pred[512,512]{0,1:T(8,128)(4,1)}, u32[]{:S(2)}) copy-start(pred[512,512]{0,1:T(8,128)(4,1)} %copy-done.21) | copy-start | bytes 786436
  155.5 3.1 %copy-start.33 = (bf16[512,192]{0,1:T(8,128)(2,1)S(1)}, bf16[512,192]{0,1:T(8,128)(2,1)}, u32[]{:S(2)}) copy-start(bf16[512,192]{0,1:T(8,128)(2,1)} %copy-done.32) | copy-start | bytes 589828
  158.6 3.6 %copy-start.37 = (bf16[512,3,64]{0,2,1:T(8,128)(2,1)}, bf16[512,3,64]{0,2,1:T(8,128)(2,1)S(1)}, u32[]{:S(2)}) copy-start(bf16[512,3,64]{0,2,1:T(8,128)(2,1)S(1)} %get-tuple-element.146) | copy-start | bytes 589828
  159.9 1.0 copy-start.29
  160.9 1.4 copy-start.4
  161.5 1.7 copy-start.34
  164.1 1.6 copy-start.31
  165.6 3.0 %copy-start.35 = (bf16[3,64,512]{2,1,0:T(8,128)(2,1)S(1)}, bf16[3,64,512]{2,1,0:T(8,128)(2,1)}, u32[]{:S(2)}) copy-start(bf16[3,64,512]{2,1,0:T(8,128)(2,1)} %copy-done.34) | copy-start | bytes 589828
  165.6 3.0 %copy-start.38 = (bf16[512,3,64]{0,2,1:T(8,128)(2,1)S(1)}, bf16[512,3,64]{0,2,1:T(8,128)(2,1)}, u32[]{:S(2)}) copy-start(bf16[512,3,64]{0,2,1:T(8,128)(2,1)} %copy-done.37) | copy-start | bytes 589828
  169.7 23.2 %copy-start.24 = (f32[128,768]{1,0:T(8,128)S(1)}, f32[128,768]{1,0:T(8,128)}, u32[]{:S(2)}) copy-start(f32[128,768]{1,0:T(8,128)} %copy-done.23) | copy-start | bytes 1179652
  192.6 3.9 %copy-start.8 = (f32[96,768]{1,0:T(8,128)S(1)}, f32[96,768]{1,0:T(8,128)}, u32[]{:S(2)}) copy-start(f32[96,768]{1,0:T(8,128)} %copy-done.7) | copy-start | bytes 884740
  192.9 4.4 %copy-start.6 = (f32[96,768]{1,0:T(8,128)S(1)}, f32[96,768]{1,0:T(8,128)}, u32[]{:S(2)}) copy-start(f32[96,768]{1,0:T(8,128)} %copy-done.5) | copy-start | bytes 884740
  (7 other events, 5.5 us)
